TPU v7x, 128 devices: a whole 4x4x4 slice. The times are simulated.
128 devices in a mesh: dp: 8 (over z_lo, x), vocab: 16 (over z_hi, y, core).
Axes of the slice: x: 4, y: 4, z: 4 (z_hi: 2, z_lo: 2; z = z_hi * 2 + z_lo), core: 2. Of those that a mesh axis runs over, the one named last changes fastest.
Arguments:
- hidden: bfloat16 [2048, 2048], P('dp'), may hold values from -40 to 40
- norm_gain: float32 [2048], replicated, may hold values from 0.1 to 1.9
- head_weight: bfloat16 [2048, 64128], P(None, 'vocab'), may hold values from -1.0617864 to 1.0617864
- teacher: bfloat16 [2048, 64128], P(('dp', 'vocab')), may hold values from -40 to 256
- labels: int32 [2048], P('dp'), may hold values from 0 to 64127
- cotangent: float32 [2048], P('dp'), may hold values from 2 to 16
Outputs:
- hidden_grad: bfloat16 [2048, 2048], P('dp', 'vocab')
- per_token_loss: float32 [2048], P('dp')
All inputs are finite; a program needn't handle non-finite values.
Results may differ from a plain program's by a relative error of at most 0.0093.
Values may be sent and summed in bfloat16 or wider, within the bound.
A program may use at most 128 MiB of HBM per device.

v0:
```python
import jax
import jax.numpy as jnp
from jax import lax
from jax.sharding import PartitionSpec as P

SOFTEN_FACTOR = 2.0
BLEND_WEIGHT = 0.5
EPSILON = 1e-05


def on_device(hidden, norm_gain, head_weight, teacher, labels, cotangent):
    shard_width = head_weight.shape[1]
    column_start = lax.axis_index("vocab") * shard_width
    target_label = lax.all_to_all(teacher, "vocab", split_axis=1, concat_axis=0, tiled=True)
    hidden_f = hidden.astype(jnp.float32)
    reciprocal = lax.rsqrt(jnp.mean(hidden_f * hidden_f, axis=1) + EPSILON)
    normed = hidden_f * reciprocal[:, None]
    features = (normed * norm_gain[None, :]).astype(jnp.bfloat16)
    student_logits = jnp.dot(features, head_weight, preferred_element_type=jnp.float32)
    target_label = target_label.astype(jnp.float32)
    column_ids = lax.broadcasted_iota(jnp.int32, student_logits.shape, 1) + column_start
    is_label = column_ids == labels[:, None]
    picked_part = jnp.sum(jnp.where(is_label, student_logits, 0.0), axis=1)
    local_student = jnp.max(student_logits, axis=1)
    local_teacher = jnp.max(target_label, axis=1)
    student_maximum, teacher_maximum = lax.pmax((local_student, local_teacher), "vocab")
    student_soft_probs = jnp.exp((student_logits - student_maximum[:, None]) / SOFTEN_FACTOR)
    hard_student = jnp.exp(student_logits - student_maximum[:, None])
    teacher_soft_probs = jnp.exp((target_label - teacher_maximum[:, None]) / SOFTEN_FACTOR)
    soft_partition_sum, total_hard, teacher_partition_sum, cross_entropy_sum, selected_logit = (
        lax.psum(
            (
                jnp.sum(student_soft_probs, axis=1),
                jnp.sum(hard_student, axis=1),
                jnp.sum(teacher_soft_probs, axis=1),
                jnp.sum(teacher_soft_probs * (target_label - student_logits), axis=1),
                picked_part,
            ),
            "vocab",
        )
    )
    student_soft = student_soft_probs / soft_partition_sum[:, None]
    student_hard = hard_student / total_hard[:, None]
    teacher_soft = teacher_soft_probs / teacher_partition_sum[:, None]
    soft_log_probs = student_maximum / SOFTEN_FACTOR + jnp.log(soft_partition_sum)
    teacher_log_probs = teacher_maximum / SOFTEN_FACTOR + jnp.log(teacher_partition_sum)
    hard_log_probs = student_maximum + jnp.log(total_hard)
    kullback_divergence = (
        cross_entropy_sum / (SOFTEN_FACTOR * teacher_partition_sum)
        - teacher_log_probs
        + soft_log_probs
    )
    per_token_loss = BLEND_WEIGHT * SOFTEN_FACTOR * SOFTEN_FACTOR * kullback_divergence + (
        1.0 - BLEND_WEIGHT
    ) * (hard_log_probs - selected_logit)
    soft_residual = student_soft - teacher_soft
    hard_residual = student_hard - is_label.astype(jnp.float32)
    logit_gradient = cotangent[:, None] * (
        BLEND_WEIGHT * SOFTEN_FACTOR * soft_residual + (1.0 - BLEND_WEIGHT) * hard_residual
    )
    logit_gradient = logit_gradient.astype(jnp.bfloat16)
    feature_count = hidden.shape[1]
    slice_width = feature_count // lax.axis_size("vocab")
    feature_start = lax.axis_index("vocab") * slice_width
    owned_rows = lax.psum_scatter(
        lax.dot_general(
            head_weight,
            logit_gradient,
            (((1,), (1,)), ((), ())),
            preferred_element_type=jnp.float32,
        ),
        "vocab",
        scatter_dimension=0,
        tiled=True,
    )
    feature_grad = owned_rows.T
    normed_part = lax.dynamic_slice_in_dim(normed, feature_start, slice_width, 1)
    gain_part = lax.dynamic_slice_in_dim(norm_gain, feature_start, slice_width, 0)
    upstream = gain_part[None, :] * feature_grad
    inner_total = lax.psum(jnp.sum(upstream * normed_part, axis=1), "vocab")
    inner_mean = inner_total / feature_count
    hidden_grad = (reciprocal[:, None] * (upstream - normed_part * inner_mean[:, None])).astype(
        jnp.bfloat16
    )
    return (hidden_grad, per_token_loss)


def solution(mesh):
    return jax.shard_map(
        on_device,
        mesh=mesh,
        in_specs=(P("dp", None), P(), P(None, "vocab"), P(("dp", "vocab"), None), P("dp"), P("dp")),
        out_specs=(P("dp", "vocab"), P("dp")),
        check_vma=False,
    )
```

profile of v0, /device:TPU:1, one launch (start us, length us, event | category | flops | bytes accessed | tf_op | source)
XLA Modules:
  0.0 260.1 jit_solution(4398936783071530586)
XLA Ops:
  7.2 4.5 %all_to_all.12 = bf16[16,16,4008]{2,1,0:T(8,128)(2,1)S(1)} reshape(bf16[16,64128]{1,0:T(8,128)(2,1)} %param.9) | data formatting | bytes 4104192 | tf_op jit(solution)/shard_map/all_to_all | solution.py:14
  11.6 0.0 copy-start
  11.6 0.0 copy-start.2
  11.7 2.5 copy.9
  14.2 9.3 %all-to-all-start = ((bf16[16,16,4008]{2,0,1:T(8,128)(2,1)}), bf16[16,16,4008]{2,0,1:T(8,128)(2,1)S(1)}, u32[]{:S(2)}, u32[]{:S(2)}) async-start(bf16[16,16,4008]{2,0,1:T(8,128)(2,1)} %copy.9), calls=%async_computation | async-start | bytes 4194304 | tf_op jit(solution)/shard_map/all_to_all | solution.py:14
  23.5 0.0 reduce-scatter.2.cloned.1.call-start
  23.5 0.0 copy-done
  23.5 0.3 fusion.7
  23.8 0.0 copy-done.2
  23.8 13.5 %fusion.24 = (f32[256]{0:T(256)S(1)}, f32[256,4008]{0,1:T(8,128)}) fusion(bf16[2048,4008]{0,1:T(8,128)(2,1)} %param.8, f32[2048]{0:T(1024)S(1)} %copy-done.2, f32[256]{0:T(256)S(1)} %add_rsqrt_fusion, bf16[256,2048]{1,0:T(8,128)(2,1)S(1)} %copy-done), kind=kOutput, calls=%fused_computation.42 | convolution fusion | flops 4205815552 | bytes 21579776 | tf_op jit(solution)/shard_map/dot_general | solution.py:19
  37.4 14.7 %all-to-all-done = bf16[16,16,4008]{2,0,1:T(8,128)(2,1)S(1)} async-done(((bf16[16,16,4008]{2,0,1:T(8,128)(2,1)}), bf16[16,16,4008]{2,0,1:T(8,128)(2,1)S(1)}, u32[]{:S(2)}, u32[]{:S(2)}) %all-to-all-start) | async-done | bytes 2052128 | tf_op jit(solution)/shard_map/all_to_all | solution.py:14
  52.1 2.4 bitcast_convert_fusion
  54.5 5.5 %copy.10 = f32[256,4008]{0,1:T(8,128)} copy(f32[256,4008]{1,0:T(8,128)} %bitcast.19) | data formatting | bytes 8208384 | tf_op jit(solution)/shard_map/convert_element_type | solution.py:20
  60.0 0.0 copy-start.1
  60.0 0.3 bitcast_reduce_fusion
  60.4 0.1 reshape.33
  60.5 33.2 %all-reduce.2 = (f32[256]{0:T(256)S(1)}, f32[256]{0:T(256)S(1)}) all-reduce(f32[256]{0:T(256)S(1)} %reshape.33, f32[256]{0:T(256)S(1)} %get-tuple-element.16), channel_id=1, replica_groups=mesh['dp'=8,'vocab'=16] {'vocab'}, use_global_device_ids=true, to_apply=%region_6.7 | all-reduce | flops 512 | bytes 4096 | tf_op jit(solution)/shard_map/pmax | solution.py:26
  93.7 0.1 sub.49
  93.8 1.0 exponential_reduce_fusion
  94.7 0.1 reduce_sum.68
  94.8 0.0 copy-done.1
  94.8 0.0 copy-start.3
  94.9 5.4 %multiply_reduce_fusion = (f32[256]{0:T(256)S(1)}, f32[256]{0:T(256)S(1)}, f32[256]{0:T(256)S(1)}, f32[256]{0:T(256)S(1)}) fusion(f32[256,4008]{0,1:T(8,128)} %copy.10, f32[256,4008]{0,1:T(8,128)} %get-tuple-element.17, f32[256]{0:T(256)S(1)} %get-tuple-element.14, s32[256]{0:T(256)S(1)} %copy-done.1, s32[4008]{0:T(1024)S(1)} %iota_add_fusion, ...), kind=kLoop, calls=%fused_computation.9 | loop fusion | flops 12311552 | bytes 8231584 | tf_op jit(solution)/shard_map/reduce_sum | solution.py:36
  100.2 34.4 %all-reduce.1 = (f32[256]{0:T(256)S(1)}, f32[256]{0:T(256)S(1)}, f32[256]{0:T(256)S(1)}) all-reduce(f32[256]{0:T(256)S(1)} %get-tuple-element.6, f32[256]{0:T(256)S(1)} %reduce_sum.68, f32[256]{0:T(256)S(1)} %get-tuple-element.7), channel_id=1, replica_groups=mesh['dp'=8,'vocab'=16] {'vocab'}, use_global_device_ids=true, to_apply=%region_10.11 | all-reduce | flops 768 | bytes 6144 | tf_op jit(solution)/shard_map/psum | solution.py:31
  134.6 0.0 copy-done.3
  134.6 12.9 %convolution_bitcast_fusion = f32[2048,256]{0,1:T(8,128)} fusion(bf16[2048,4008]{0,1:T(8,128)(2,1)} %param.8, f32[256,4008]{0,1:T(8,128)} %copy.10, f32[256,4008]{0,1:T(8,128)} %get-tuple-element.17, s32[256]{0:T(256)S(1)} %copy-done.1, f32[256]{0:T(256)S(1)} %get-tuple-element.11, f32[256]{0:T(256)S(1)} %get-tuple-element.12, ...), kind=kOutput, calls=%fused_computation.14 | convolution fusion | flops 4218083328 | bytes 26745504 | tf_op jit(solution)/shard_map/dot_general | solution.py:66
  147.5 0.0 reduce-scatter.2.cloned.1.call-update
  147.6 0.1 dynamic_slice.6
  147.6 0.2 convert_multiply_fusion
  147.8 67.1 %reduce-scatter.2.cloned.1.call-done = f32[128,256]{0,1:T(8,128)} async-done(((f32[2048,256]{0,1:T(8,128)}), f32[128,256]{0,1:T(8,128)}) %reduce-scatter.2.cloned.1.call-update) | async-done | bytes 131088 | tf_op jit(solution)/shard_map/reduce_scatter | solution.py:65
  214.9 1.0 fusion.20
  216.0 35.0 %all-reduce = (f32[256]{0:T(256)S(1)}, f32[256]{0:T(256)S(1)}, f32[256]{0:T(256)S(1)}) all-reduce(f32[256]{0:T(256)S(1)} %fusion.20, f32[256]{0:T(256)S(1)} %get-tuple-element.5, f32[256]{0:T(256)S(1)} %get-tuple-element.4), channel_id=1, replica_groups=mesh['dp'=8,'vocab'=16] {'vocab'}, use_global_device_ids=true, to_apply=%region_13.14 | all-reduce | flops 768 | bytes 6144 | tf_op jit(solution)/shard_map/psum | solution.py:80
  251.0 0.6 multiply_add_fusion
  251.6 1.7 fusion.22
  (2 shorter events, 0.0 us)
Async XLA Ops:
  11.6 11.9 %copy-start = (bf16[256,2048]{1,0:T(8,128)(2,1)S(1)}, bf16[256,2048]{1,0:T(8,128)(2,1)}, u32[]{:S(2)}) copy-start(bf16[256,2048]{1,0:T(8,128)(2,1)} %param.6) | copy-start | bytes 3145732
  11.6 12.2 %copy-start.2 = (f32[2048]{0:T(1024)S(1)}, f32[2048]{0:T(1024)}, u32[]{:S(2)}) copy-start(f32[2048]{0:T(1024)} %param.7) | copy-start | bytes 24580
  14.2 37.9 %all-to-all-start = ((bf16[16,16,4008]{2,0,1:T(8,128)(2,1)}), bf16[16,16,4008]{2,0,1:T(8,128)(2,1)S(1)}, u32[]{:S(2)}, u32[]{:S(2)}) async-start(bf16[16,16,4008]{2,0,1:T(8,128)(2,1)} %copy.9), calls=%async_computation | async-start | bytes 4194304 | tf_op jit(solution)/shard_map/all_to_all | solution.py:14
  23.5 191.5 %reduce-scatter.2.cloned.1.call-start = ((), (), s32[]{:S(2)}) async-start(), calls=%async_computation.2 | async-start | bytes 2228224 | tf_op jit(solution)/shard_map/reduce_scatter | solution.py:65
  60.0 34.8 %copy-start.1 = (s32[256]{0:T(256)S(1)}, s32[256]{0:T(256)}, u32[]{:S(2)}) copy-start(s32[256]{0:T(256)} %param.10) | copy-start | bytes 3076
  94.8 39.8 %copy-start.3 = (f32[256]{0:T(256)S(1)}, f32[256]{0:T(256)}, u32[]{:S(2)}) copy-start(f32[256]{0:T(256)} %param.11) | copy-start | bytes 3076
Sparse Core Ops, SparseCore 0:
  147.7 67.2 reduce-scatter.1
where the time goes:
time: 261 us; the launch traced here: 260 us
  blocking collectives  103 us (39%)
  waiting for transfers between devices  81.8 us (31%)
  matrix products  26.4 us (10%)
  between operations  14.1 us (5%)
  local copies, waits for them, and re-layouts  12.9 us (5%)
  other arithmetic  12.8 us (5%)
  starting transfers between devices  9.34 us (4%)
    reduce_scatter x1, waiting for transfers between devices, on_device(): lax.psum_scatter(lax.dot_general(head_weight, logit_gradient, (((1,), (1,...  67.1 us
    psum x1, blocking collectives, on_device(): inner_total = lax.psum(jnp.sum(upstream * normed_part, axis=1), 'vocab')  35 us
    psum x1, blocking collectives, on_device(): lax.psum((jnp.sum(student_soft_probs, axis=1), jnp.sum(hard_student, axis...  34.4 us
    pmax x1, blocking collectives, on_device(): lax.pmax((local_student, local_teacher), 'vocab')  33.2 us
    all_to_all x1, waiting for transfers between devices, on_device(): lax.all_to_all(teacher, 'vocab', split_axis=1, concat_axis=0, tiled=True)  14.7 us
    dot_general x1, matrix products, on_device(): jnp.dot(features, head_weight, preferred_element_type=jnp.float32)  13.5 us
    dot_general x1, matrix products, on_device(): lax.dot_general(head_weight, logit_gradient, (((1,), (1,)), ((), ())), pr...  12.9 us
    all_to_all x1, starting transfers between devices, on_device(): lax.all_to_all(teacher, 'vocab', split_axis=1, concat_axis=0, tiled=True)  9.3 us
  transfers between devices with their start and end apart: 2, of which 2 were waited for; matrix products, arithmetic and copies ran while one was open for 5% of the time, Pallas kernels for 0%

commit v1 on v0

v1 whole, which is shorter than its diff:
```python
import jax
import jax.numpy as jnp
from jax import lax
from jax.experimental import pallas as pl
from jax.experimental.pallas import tpu as pltpu
from jax.sharding import PartitionSpec as P

EPSILON = 1e-05
MESH = pl.DeviceIdType.MESH
F32 = jnp.float32
BF16 = jnp.bfloat16

N = 16
TOK = 256
ROWS = TOK // N
D = 2048
VOCAB = 64128
SHARD = VOCAB // N
LANES = 128
TILES = 32
PAD = TILES * LANES
VTILES = VOCAB // LANES
VALID = SHARD - (TILES - 1) * LANES
PIECES = ((0, 9), (9, 8), (17, 8), (25, 8))
BLOCK = 512
BLOCKS = PAD // BLOCK
BLOCK_TILES = BLOCK // LANES
LOG2E = 1.4426950408889634
LN2 = 0.6931471805599453
RELAYED = (
    (2, 2, 0, 1, 1), (2, 2, 1, 3, 3),
    (0, 2, 0, 0, 1), (0, 2, 1, 0, 3),
    (1, 2, 0, 0, 1), (1, 2, 1, 0, 3),
    (3, 2, 0, 0, 1), (3, 2, 1, 0, 3),
    (2, 0, 0, 1, 0), (2, 0, 1, 3, 0),
)
OWN = D // N
CHIPS = N // 2
FULL_W = (SHARD // 16) * 16


def kernel(
    hidden, gain, wt, teacher, labels, cot,
    out, loss,
    hid, w, t_v, land, relay, feats, logits, fg, g_v,
    lse_src, lse_land, st_src, st_land, fin_src, fin_land,
    cx_src, cx_land, rs_src, rs_land,
    a_b, b_b, c_b, l_b, r_b, mx_b, soft_b, hard_b, pick_b, cross_b, inner_b, rows_v,
    loc_sem, w_sem, ts, tr, fs, ft, ms, mr, cs, cr, rs, rr,
):
    me = lax.axis_index("vocab")
    chip = lax.div(me, 2)
    core = lax.rem(me, 2)
    width = lax.axis_size("dp") // 2
    x = lax.rem(lax.axis_index("dp"), width)
    y = lax.rem(chip, 4)
    z = lax.div(me, 8) * 2 + lax.div(lax.axis_index("dp"), width)

    def group_index(dy, dz, c):
        return (lax.div(lax.rem(z + dz, 4), 2) * 4 + lax.rem(y + dy, 4)) * 2 + c

    def device(dy, dz, c):
        return {
            "dp": lax.rem(z + dz, 2) * width + x,
            "vocab": group_index(dy, dz, c),
        }

    lane = lax.broadcasted_iota(jnp.int32, (ROWS, LANES), 1)
    places = [(lane + i * LANES).astype(F32) for i in range(BLOCK_TILES)]
    my_rows = pl.ds(pl.multiple_of(me * ROWS, ROWS), ROWS)

    hid_copy = pltpu.make_async_copy(hidden, hid, loc_sem.at[0])
    hid_copy.start()
    t_copy = pltpu.make_async_copy(teacher, t_v, loc_sem.at[1])
    t_copy.start()
    w[FULL_W:PAD, :] = jnp.zeros((PAD - FULL_W, D), BF16)
    w_copies = []
    for c in range(BLOCKS):
        lo, hi = c * BLOCK, min((c + 1) * BLOCK, SHARD)
        copy = pltpu.make_async_copy(wt.at[lo:hi], w.at[lo:hi], w_sem.at[c])
        copy.start()
        w_copies.append(copy)

    barrier = pltpu.get_barrier_semaphore()

    def greet(k, _):
        pl.semaphore_signal(
            barrier, inc=1, device_id={"vocab": lax.rem(me + k, N)}, device_id_type=MESH
        )
        return 0

    lax.fori_loop(1, N, greet, 0)
    for dz in (1, 3):
        for dy in (0, 1, 3):
            for c in (0, 1):
                pl.semaphore_signal(
                    barrier, inc=1, device_id=device(dy, dz, c), device_id_type=MESH
                )
    pl.semaphore_wait(barrier, N - 1 + 12)

    def remote_to(src, dst, send_sem, recv_sem, target):
        return pltpu.make_async_remote_copy(
            src_ref=src, dst_ref=dst, send_sem=send_sem, recv_sem=recv_sem,
            device_id=target, device_id_type=MESH,
        )

    def remote(src, dst, send_sem, recv_sem, d):
        return remote_to(src, dst, send_sem, recv_sem, {"vocab": d})

    def columns_of(c):
        first, count = PIECES[c]
        return slice(first * LANES, (first + count) * LANES)

    def piece_copies(d, c, into):
        first, count = PIECES[c]
        base = lax.div(d * SHARD, LANES)
        spans = [(base + first, first, count)]
        if first + count > TILES:
            spans = [
                (base + first, first, count - 1),
                (jnp.minimum(base + TILES, VTILES - 1), TILES, 1),
            ]
        for start, at, tiles in spans:
            yield (
                teacher.at[:, pl.ds(pl.multiple_of(start * LANES, LANES), tiles * LANES)],
                into(slice(at * LANES, (at + tiles) * LANES)),
            )

    for c in range(len(PIECES)):
        for p, (dy, dz, dc, ry, rz) in enumerate(RELAYED):
            d = group_index(dy, dz, dc)
            for src, dst in piece_copies(d, c, lambda cols, p=p: relay.at[p, :, cols]):
                remote_to(src, dst, ts.at[c], ft.at[c], device(ry, rz, core)).start()
        for dy, dc in ((1, 0), (3, 0), (1, 1), (3, 1)):
            d = group_index(dy, 0, dc)
            for src, dst in piece_copies(d, c, lambda cols: land.at[my_rows, cols]):
                remote(src, dst, ts.at[c], tr.at[c], d).start()
        sibling = chip * 2 + (1 - core)
        for src, dst in piece_copies(sibling, c, lambda cols: land.at[my_rows, cols]):
            remote(src, dst, ts.at[c], tr.at[c], sibling).start()
        for src, dst in piece_copies(me, c, lambda cols: land.at[my_rows, cols]):
            pltpu.make_async_copy(src, dst, tr.at[c]).start()

    def forward_pieces(c):
        cols = columns_of(c)
        wait_for(relay.at[:, :, cols], ft.at[c])
        for p, (dy, dz, dc, ry, rz) in enumerate(RELAYED):
            origin = group_index(4 - ry, 4 - rz, core)
            rows = pl.ds(pl.multiple_of(origin * ROWS, ROWS), ROWS)
            remote_to(
                relay.at[p, :, cols], land.at[rows, cols], fs.at[c], tr.at[c],
                device(4 + dy - ry, 4 + dz - rz, dc),
            ).start()

    def wait_for(ref, sem):
        pltpu.make_async_copy(ref, ref, sem).wait()

    t_copy.wait()
    wide = 33
    steps = VTILES // wide
    rest = VTILES - steps * wide

    def t_tiles(i, count):
        start = i * (wide * LANES)
        return [
            t_v[:, pl.ds(pl.multiple_of(start + t * LANES, LANES), LANES)] for t in range(count)
        ]

    def tile_max(i, accs, count=wide):
        accs = list(accs)
        for t, x in enumerate(t_tiles(i, count)):
            accs[t % 4] = jnp.maximum(accs[t % 4], x)
        return tuple(accs)

    accs = tile_max(steps, (t_v[:, :LANES],) * 4, rest)
    accs = lax.fori_loop(0, steps, tile_max, accs)
    top = jnp.maximum(jnp.maximum(accs[0], accs[1]), jnp.maximum(accs[2], accs[3]))
    top = (0.5 * LOG2E) * jnp.max(top.astype(F32), axis=1, keepdims=True)

    def tile_sum(i, accs, count=wide):
        accs = list(accs)
        for t, x in enumerate(t_tiles(i, count)):
            accs[t % 4] = accs[t % 4] + jnp.exp2((0.5 * LOG2E) * x.astype(F32) - top)
        return tuple(accs)

    accs = tile_sum(steps, (jnp.zeros((ROWS, LANES), F32),) * 4, rest)
    accs = lax.fori_loop(0, steps, tile_sum, accs)
    total = jnp.sum((accs[0] + accs[1]) + (accs[2] + accs[3]), axis=1, keepdims=True)
    lse_src[...] = jnp.broadcast_to(top + LOG2E * jnp.log(total), (ROWS, LANES))

    def send_lse(k, _):
        remote(
            lse_src, lse_land.at[my_rows, :], ms.at[0], mr.at[0], lax.rem(me + k, N)
        ).start()
        return 0

    pltpu.make_async_copy(lse_src, lse_land.at[my_rows, :], mr.at[0]).start()
    lax.fori_loop(1, N, send_lse, 0)

    forward_pieces(0)

    local = labels[...] - me * SHARD
    inside = jnp.logical_and(local >= 0, local < SHARD)
    local = jnp.where(inside, local, -1).astype(F32)
    columns = jnp.concatenate(
        [local, cot[...], jnp.zeros((LANES - 2, TOK), F32)], axis=0
    ).T
    l_b[...] = jnp.broadcast_to(columns[:, 0:1], (TOK, LANES))
    c_b[...] = jnp.broadcast_to(columns[:, 1:2], (TOK, LANES))

    hid_copy.wait()

    tall = 64

    def make_features(s, _):
        at = pl.ds(pl.multiple_of(s * tall, tall), tall)
        acc = jnp.zeros((tall, LANES), F32)
        for t in range(D // LANES):
            h = hid[at, t * LANES : (t + 1) * LANES].astype(F32)
            acc = acc + h * h
        r = lax.rsqrt(jnp.sum(acc, axis=1, keepdims=True) * (1.0 / D) + EPSILON)
        r = jnp.broadcast_to(r, (tall, LANES))
        r_b[at, :] = r
        for t in range(D // LANES):
            cols = slice(t * LANES, (t + 1) * LANES)
            feats[at, cols] = ((hid[at, cols].astype(F32) * r) * gain[:, cols]).astype(BF16)
        return 0

    lax.fori_loop(0, TOK // tall, make_features, 0)

    zeros = jnp.zeros((TOK, LANES), F32)
    mx_b[...] = jnp.full((TOK, LANES), -1e30, F32)
    soft_b[...] = zeros
    hard_b[...] = zeros
    pick_b[...] = zeros
    for c in range(BLOCKS):
        w_copies[c].wait()

    forward_pieces(1)

    def forward(c):
        at = pl.ds(pl.multiple_of(c * BLOCK, BLOCK), BLOCK)
        logits[c] = lax.dot_general(
            feats[...], w[at, :], (((1,), (1,)), ((), ())), preferred_element_type=F32
        )

    def student_sums(c, s):
        at = pl.ds(s * ROWS, ROWS)
        tiles = [logits[c, at, i * LANES : (i + 1) * LANES] for i in range(BLOCK_TILES)]
        top = mx_b[at, :]
        label = l_b[at, :] - jnp.float32(c * BLOCK)
        new = jnp.maximum(
            jnp.maximum(top, tiles[0]), jnp.maximum(jnp.maximum(tiles[1], tiles[2]), tiles[3])
        )
        mx_b[at, :] = new
        scale = jnp.exp2((0.5 * LOG2E) * (top - new))
        soft = soft_b[at, :] * scale
        hard = hard_b[at, :] * (scale * scale)
        picked = pick_b[at, :]
        for i, v in enumerate(tiles):
            e = jnp.exp2((0.5 * LOG2E) * (v - new))
            soft = soft + e
            hard = hard + e * e
            picked = picked + jnp.where(places[i] == label, v, 0.0)
        soft_b[at, :] = soft
        hard_b[at, :] = hard
        pick_b[at, :] = picked

    forward(0)

    def forward_step(c, _):
        @pl.when(c == 4)
        def _():
            forward_pieces(2)

        for s in range(TOK // ROWS):
            student_sums(c - 1, s)
        forward(c)
        return 0

    lax.fori_loop(1, BLOCKS, forward_step, 0)
    last = slice((BLOCK_TILES - 1) * LANES, BLOCK)
    wide_lane = lax.broadcasted_iota(jnp.int32, (TOK, LANES), 1)
    logits[BLOCKS - 1, :, last] = jnp.where(
        wide_lane < VALID, logits[BLOCKS - 1, :, last], -1e30
    )
    for s in range(TOK // ROWS):
        student_sums(BLOCKS - 1, s)
    forward_pieces(3)

    top = mx_b[...]
    m = jnp.max(top, axis=1, keepdims=True)
    scale = jnp.exp2((0.5 * LOG2E) * (top - m))
    soft = jnp.sum(soft_b[...] * scale, axis=1, keepdims=True)
    hard = jnp.sum(hard_b[...] * (scale * scale), axis=1, keepdims=True)
    picked = jnp.sum(pick_b[...], axis=1, keepdims=True)
    stat = jnp.where(wide_lane == 0, m, jnp.where(wide_lane == 1, soft, hard))
    st_src[...] = jnp.where(wide_lane == 3, picked, stat).T[0:8, :]

    def send_stats(k, _):
        remote(
            st_src, st_land.at[me], ms.at[1], mr.at[1], lax.rem(me + k, N)
        ).start()
        return 0

    pltpu.make_async_copy(st_src, st_land.at[me], mr.at[1]).start()
    lax.fori_loop(1, N, send_stats, 0)
    wait_for(st_land, mr.at[1])

    top = st_land[0, 0:1, :]
    for s in range(1, N):
        top = jnp.maximum(top, st_land[s, 0:1, :])
    soft = jnp.zeros((1, TOK), F32)
    hard = jnp.zeros((1, TOK), F32)
    picked = jnp.zeros((1, TOK), F32)
    for s in range(N):
        stat = st_land[s]
        scale = jnp.exp2((0.5 * LOG2E) * (stat[0:1] - top))
        soft = soft + stat[1:2] * scale
        hard = hard + stat[2:3] * (scale * scale)
        picked = picked + stat[3:4]
    lse_soft = 0.5 * top + jnp.log(soft)
    rows_v[0:1, :] = lse_soft
    rows_v[1:2, :] = top + jnp.log(hard)
    rows_v[2:3, :] = picked
    columns = jnp.concatenate(
        [
            LOG2E * lse_soft,
            0.5 * cot[...] * (soft * soft) / hard,
            jnp.zeros((LANES - 2, TOK), F32),
        ],
        axis=0,
    ).T
    a_b[...] = jnp.broadcast_to(columns[:, 0:1], (TOK, LANES))
    b_b[...] = jnp.broadcast_to(columns[:, 1:2], (TOK, LANES))
    cross_b[...] = zeros
    inner_b[...] = zeros
    for n in range(CHIPS):
        fg[n] = jnp.zeros((TOK, 2 * OWN), F32)
    wait_for(lse_land, mr.at[0])

    off = lax.rem(me * SHARD, LANES)
    shift = lax.rem(LANES - off, LANES)
    keep = lane < LANES - off
    partner = chip * 2 + (1 - core)

    def wait_piece(c):
        wait_for(land.at[:, columns_of(c)], tr.at[c])

    def gradient(c, s):
        at = pl.ds(s * ROWS, ROWS)
        slot = lax.rem(c, 2)
        lse_s, b, ct = a_b[at, :], b_b[at, :], c_b[at, :]
        label = l_b[at, :] - jnp.float32(c * BLOCK)
        lse_t = lse_land[at, :]
        half = 0.5 * ct
        cross, inner = cross_b[at, :], inner_b[at, :]

        def turned(i):
            start = pl.multiple_of(c * BLOCK + i * LANES, LANES)
            return pltpu.roll(land[at, pl.ds(start, LANES)].astype(F32), shift, 1)

        here = turned(0)
        for i in range(BLOCK_TILES):
            after = turned(i + 1)
            x = jnp.where(keep, here, after)
            here = after
            v = logits[c, at, i * LANES : (i + 1) * LANES]
            p = jnp.exp2((0.5 * LOG2E) * x - lse_t)
            e = jnp.exp2((0.5 * LOG2E) * v - lse_s)
            if i == BLOCK_TILES - 1:
                p = jnp.where(lane < SHARD - i * LANES - c * BLOCK, p, 0.0)
            cross = cross + p * (x - v)
            g = e * (ct + e * b) - ct * p
            g = g - jnp.where(places[i] == label, half, 0.0)
            g = g.astype(BF16)
            g_v[slot, at, i * LANES : (i + 1) * LANES] = g
            inner = inner + g.astype(F32) * v
        cross_b[at, :] = cross
        inner_b[at, :] = inner

    def backward(c, n):
        rows = pl.ds(pl.multiple_of(c * BLOCK, BLOCK), BLOCK)
        at = pl.ds(pl.multiple_of(n * (2 * OWN), 2 * OWN), 2 * OWN)
        part = jnp.dot(g_v[lax.rem(c, 2)], w[rows, at], preferred_element_type=F32)
        return fg[n] + part

    wait_piece(0)
    for s in range(TOK // ROWS):
        gradient(0, s)

    def step(c, _):
        for p in range(1, len(PIECES)):

            @pl.when(c + 1 == 2 * p)
            def _():
                wait_piece(p)

        for s in range(TOK // ROWS):
            gradient(c + 1, s)
        for n in range(CHIPS):
            fg[n] = backward(c, n)
        return 0

    lax.fori_loop(0, BLOCKS - 1, step, 0)

    cross = jnp.sum(cross_b[...], axis=1, keepdims=True)
    inner = jnp.sum(inner_b[...], axis=1, keepdims=True)
    stat = jnp.where(wide_lane == 0, cross, inner)
    fin_src[...] = jnp.where(wide_lane == 2, LN2 * lse_land[...], stat).T[0:8, :]

    def send_final(k, _):
        remote(
            fin_src, fin_land.at[me], ms.at[2], mr.at[2], lax.rem(me + k, N)
        ).start()
        return 0

    pltpu.make_async_copy(fin_src, fin_land.at[me], mr.at[2]).start()
    lax.fori_loop(1, N, send_final, 0)

    for k in range(CHIPS):
        n = lax.rem(chip + 1 + k, CHIPS)
        part = backward(BLOCKS - 1, n)
        fg[n] = part
        theirs = jnp.where(core == 0, part[:, OWN:], part[:, :OWN])
        cx_src[n] = theirs.astype(BF16)
        remote(cx_src.at[n], cx_land.at[n], cs.at[0], cr.at[n], partner).start()

    def own_half(n):
        part = fg[n]
        half = jnp.where(core == 0, part[:, :OWN], part[:, OWN:])
        return half + cx_land[n].astype(F32)

    def share(k, _):
        n = lax.rem(chip + 1 + k, CHIPS)
        wait_for(cx_land.at[n], cr.at[n])
        rs_src[n] = own_half(n).astype(BF16)
        remote(rs_src.at[n], rs_land.at[chip], rs, rr, n * 2 + core).start()
        return 0

    lax.fori_loop(0, CHIPS - 1, share, 0)
    wait_for(cx_land.at[chip], cr.at[chip])
    fg[chip, :, :OWN] = own_half(chip)

    wait_for(fin_land, mr.at[2])
    cross = jnp.zeros((1, TOK), F32)
    inner = jnp.zeros((1, TOK), F32)
    for s in range(N):
        stat = fin_land[s]
        cross = cross + stat[0:1]
        inner = inner + stat[1:2]
    kl = 0.5 * cross - fin_src[2:3, :] + rows_v[0:1, :]
    loss[...] = 2.0 * kl + 0.5 * (rows_v[1:2, :] - rows_v[2:3, :])
    columns = jnp.concatenate(
        [inner * (1.0 / D), jnp.zeros((LANES - 1, TOK), F32)], axis=0
    ).T
    a_b[...] = jnp.broadcast_to(columns[:, 0:1], (TOK, LANES))

    wait_for(rs_land.at[0 : CHIPS - 1], rr)
    mine = pl.ds(pl.multiple_of(me * OWN, OWN), OWN)
    total = fg[chip, :, :OWN]
    for k in range(1, CHIPS):
        total = total + rs_land[lax.rem(chip + k, CHIPS)].astype(F32)
    r = r_b[...]
    normed = hid[:, mine].astype(F32) * r
    out[...] = (r * (gain[:, mine] * total - normed * a_b[...])).astype(BF16)

    for c in range(len(PIECES)):
        wait_for(land.at[0 : TOK - ROWS, columns_of(c)], ts.at[c])
        wait_for(relay.at[:, :, columns_of(c)], fs.at[c])
    wait_for(lse_land.at[0 : TOK - ROWS], ms.at[0])
    wait_for(st_land.at[0 : N - 1], ms.at[1])
    wait_for(fin_land.at[0 : N - 1], ms.at[2])
    wait_for(cx_src, cs.at[0])
    wait_for(rs_src.at[0 : CHIPS - 1], rs)


def on_device(hidden, norm_gain, head_weight, teacher, labels, cotangent):
    vmem = pl.BlockSpec(memory_space=pltpu.VMEM)
    hbm = pl.BlockSpec(memory_space=pl.ANY)
    dma = pltpu.SemaphoreType.DMA
    column = pltpu.VMEM((TOK, LANES), F32)
    grad, loss = pl.pallas_call(
        kernel,
        out_shape=(
            jax.ShapeDtypeStruct((TOK, OWN), BF16),
            jax.ShapeDtypeStruct((1, TOK), F32),
        ),
        in_specs=[hbm, vmem, hbm, hbm, vmem, vmem],
        out_specs=(vmem, vmem),
        scratch_shapes=[
            pltpu.VMEM((TOK, D), BF16),
            pltpu.VMEM((PAD, D), BF16),
            pltpu.VMEM((ROWS, VOCAB), BF16),
            pltpu.VMEM((TOK, PAD + LANES), BF16),
            pltpu.VMEM((len(RELAYED), ROWS, PAD + LANES), BF16),
            pltpu.VMEM((TOK, D), BF16),
            pltpu.VMEM((BLOCKS, TOK, BLOCK), F32),
            pltpu.VMEM((CHIPS, TOK, 2 * OWN), F32),
            pltpu.VMEM((2, TOK, BLOCK), BF16),
            pltpu.VMEM((ROWS, LANES), F32),
            column,
            pltpu.VMEM((8, TOK), F32),
            pltpu.VMEM((N, 8, TOK), F32),
            pltpu.VMEM((8, TOK), F32),
            pltpu.VMEM((N, 8, TOK), F32),
            pltpu.VMEM((CHIPS, TOK, OWN), BF16),
            pltpu.VMEM((CHIPS, TOK, OWN), BF16),
            pltpu.VMEM((CHIPS, TOK, OWN), BF16),
            pltpu.VMEM((CHIPS, TOK, OWN), BF16),
            column, column, column, column, column, column,
            column, column, column, column, column,
            pltpu.VMEM((8, TOK), F32),
            dma((2,)), dma((BLOCKS,)), dma((len(PIECES),)), dma((len(PIECES),)), dma((len(PIECES),)), dma((len(PIECES),)),
            dma((3,)), dma((3,)), dma((1,)), dma((CHIPS,)), dma, dma,
        ],
        compiler_params=pltpu.CompilerParams(
            collective_id=0, has_side_effects=True, vmem_limit_bytes=56 * 1024 * 1024
        ),
        cost_estimate=pl.CostEstimate(
            flops=4 * TOK * D * SHARD, bytes_accessed=20_000_000, transcendentals=3_000_000
        ),
    )(
        hidden,
        norm_gain.reshape(1, D),
        head_weight.T,
        teacher,
        labels.reshape(1, TOK),
        cotangent.reshape(1, TOK),
    )
    return grad, loss.reshape(TOK)


def solution(mesh):
    return jax.shard_map(
        on_device,
        mesh=mesh,
        in_specs=(P("dp", None), P(), P(None, "vocab"), P(("dp", "vocab"), None), P("dp"), P("dp")),
        out_specs=(P("dp", "vocab"), P("dp")),
        check_vma=False,
    )
```

time: 261 us -> 63 us (0.24)
  blocking collectives: 103 us -> 0 us
  waiting for transfers between devices: 81.8 us -> 0 us
  Pallas kernels: 0 us -> 59.5 us
  matrix products: 26.4 us -> 0 us
  between operations: 14.1 us -> 0.64 us
  other arithmetic: 12.8 us -> 0 us
  local copies, waits for them, and re-layouts: 12.9 us -> 2.67 us
  starting transfers between devices: 9.34 us -> 0 us
    psum x2 -> x0, blocking collectives: 69.4 us -> none  [the longest x1 35 us: on_device(): inner_total = lax.psum(jnp.sum(upstream * normed_part, axis=1), 'vocab')]
    reduce_scatter x1 -> x0, waiting for transfers between devices: 67.1 us -> none  [on_device(): lax.psum_scatter(lax.dot_general(head_weight, logit_gradient, (((1,), (1,...]
    pallas_call x0 -> x1, Pallas kernels: none -> 59.5 us  [on_device(): pl.pallas_call(kernel, out_shape=(jax.ShapeDtypeStruct((TOK, OWN), BF16),...]
    pmax x1 -> x0, blocking collectives: 33.2 us -> none  [on_device(): lax.pmax((local_student, local_teacher), 'vocab')]
    dot_general x2 -> x0, matrix products: 26.4 us -> none  [the longest x1 13.5 us: on_device(): jnp.dot(features, head_weight, preferred_element_type=jnp.float32)]
    all_to_all x1 -> x0, waiting for transfers between devices: 14.7 us -> none  [on_device(): lax.all_to_all(teacher, 'vocab', split_axis=1, concat_axis=0, tiled=True)]
    all_to_all x1 -> x0, starting transfers between devices: 9.3 us -> none  [on_device(): lax.all_to_all(teacher, 'vocab', split_axis=1, concat_axis=0, tiled=True)]
    reduce_sum x4 -> x0, other arithmetic: 7.62 us -> none  [the longest x1 5.37 us: on_device(): jnp.sum(teacher_soft_probs * (target_label - student_logits), axis=1)]
  transfers between devices with their start and end apart: 2 -> 0, of which waited for: 2 -> 0; matrix products, arithmetic and copies ran while one was open for 5% -> 0% of each run, Pallas kernels for 0% -> 0%
where the time goes in v1:
time: 63 us; the launch traced here: 62.8 us
  Pallas kernels  59.5 us (94%)
  local copies, waits for them, and re-layouts  2.67 us (4%)
  between operations  0.64 us (1%)
    pallas_call x1, Pallas kernels, on_device(): pl.pallas_call(kernel, out_shape=(jax.ShapeDtypeStruct((TOK, OWN), BF16),...  59.5 us
    unnamed x2, local copies, waits for them, and re-layouts  2.67 us

profile of v1, /device:TPU:1, one launch (start us, length us, event | category | flops | bytes accessed | tf_op | source)
XLA Modules:
  0.0 62.8 jit_solution(17178282518256794786)
XLA Ops:
  0.6 59.5 %shard_map.77 = (bf16[256,128]{1,0:T(8,128)(2,1)}, f32[1,256]{1,0:T(1,128)}) custom-call(bf16[256,2048]{1,0:T(8,128)(2,1)} %hidden.1, f32[1,2048]{1,0:T(1,128)} %bitcast.7, bf16[4008,2048]{1,0:T(8,128)(2,1)} %bitcast.6, bf16[16,64128]{1,0:T(8,128)(2,1)} %teacher.1, s32[1,256]{1,0:T(1,128)} %bitcast.8, f32[1,256]{1,0:T(1,128)} %bitcast.9), custom_call_target="tpu_custom_call" | custom-call | flops 8405385216 | bytes 20000000 | tf_op jit(solution)/shard_map/pallas_call | solution.py:483
  60.1 1.5 %copy.10 = bf16[256,128]{1,0:T(8,128)(2,1)} copy(bf16[256,128]{1,0:T(8,128)(2,1)} %get-tuple-element.8) | data formatting | bytes 131072
  61.6 1.2 %copy.11 = f32[256]{0:T(256)} copy(f32[256]{0:T(256)} %bitcast.5) | data formatting | bytes 2048

commit v2 on v1

--- a/solution.py
+++ b/solution.py
@@ -25,15 +25,10 @@
 BLOCK = 512
 BLOCKS = PAD // BLOCK
 BLOCK_TILES = BLOCK // LANES
+FWD = 1024
+FWDS = PAD // FWD
 LOG2E = 1.4426950408889634
 LN2 = 0.6931471805599453
-RELAYED = (
-    (2, 2, 0, 1, 1), (2, 2, 1, 3, 3),
-    (0, 2, 0, 0, 1), (0, 2, 1, 0, 3),
-    (1, 2, 0, 0, 1), (1, 2, 1, 0, 3),
-    (3, 2, 0, 0, 1), (3, 2, 1, 0, 3),
-    (2, 0, 0, 1, 0), (2, 0, 1, 3, 0),
-)
 OWN = D // N
 CHIPS = N // 2
 FULL_W = (SHARD // 16) * 16
@@ -42,29 +37,15 @@
 def kernel(
     hidden, gain, wt, teacher, labels, cot,
     out, loss,
-    hid, w, t_v, land, relay, feats, logits, fg, g_v,
+    hid, w, t_v, land, feats, logits, fg, g_now, g_next,
     lse_src, lse_land, st_src, st_land, fin_src, fin_land,
     cx_src, cx_land, rs_src, rs_land,
     a_b, b_b, c_b, l_b, r_b, mx_b, soft_b, hard_b, pick_b, cross_b, inner_b, rows_v,
-    loc_sem, w_sem, ts, tr, fs, ft, ms, mr, cs, cr, rs, rr,
+    loc_sem, w_sem, ts, tr, ms, mr, cs, cr, rs, rr,
 ):
     me = lax.axis_index("vocab")
     chip = lax.div(me, 2)
     core = lax.rem(me, 2)
-    width = lax.axis_size("dp") // 2
-    x = lax.rem(lax.axis_index("dp"), width)
-    y = lax.rem(chip, 4)
-    z = lax.div(me, 8) * 2 + lax.div(lax.axis_index("dp"), width)
-
-    def group_index(dy, dz, c):
-        return (lax.div(lax.rem(z + dz, 4), 2) * 4 + lax.rem(y + dy, 4)) * 2 + c
-
-    def device(dy, dz, c):
-        return {
-            "dp": lax.rem(z + dz, 2) * width + x,
-            "vocab": group_index(dy, dz, c),
-        }
-
     lane = lax.broadcasted_iota(jnp.int32, (ROWS, LANES), 1)
     places = [(lane + i * LANES).astype(F32) for i in range(BLOCK_TILES)]
     my_rows = pl.ds(pl.multiple_of(me * ROWS, ROWS), ROWS)
@@ -90,67 +71,45 @@
         return 0
 
     lax.fori_loop(1, N, greet, 0)
-    for dz in (1, 3):
-        for dy in (0, 1, 3):
-            for c in (0, 1):
-                pl.semaphore_signal(
-                    barrier, inc=1, device_id=device(dy, dz, c), device_id_type=MESH
-                )
-    pl.semaphore_wait(barrier, N - 1 + 12)
-
-    def remote_to(src, dst, send_sem, recv_sem, target):
+    pl.semaphore_wait(barrier, N - 1)
+
+    def piece_refs(d, first, count):
+        base = lax.div(d * SHARD, LANES) + first
+        if first + count > TILES:
+            count = count - 1
+        src = teacher.at[:, pl.ds(pl.multiple_of(base * LANES, LANES), count * LANES)]
+        dst = land.at[my_rows, first * LANES : (first + count) * LANES]
+        return src, dst
+
+    def last_refs(d):
+        base = jnp.minimum(lax.div(d * SHARD, LANES) + TILES, VTILES - 1)
+        src = teacher.at[:, pl.ds(pl.multiple_of(base * LANES, LANES), LANES)]
+        dst = land.at[my_rows, TILES * LANES : (TILES + 1) * LANES]
+        return src, dst
+
+    def remote(src, dst, send_sem, recv_sem, d):
         return pltpu.make_async_remote_copy(
             src_ref=src, dst_ref=dst, send_sem=send_sem, recv_sem=recv_sem,
-            device_id=target, device_id_type=MESH,
+            device_id={"vocab": d}, device_id_type=MESH,
         )
 
-    def remote(src, dst, send_sem, recv_sem, d):
-        return remote_to(src, dst, send_sem, recv_sem, {"vocab": d})
-
-    def columns_of(c):
-        first, count = PIECES[c]
-        return slice(first * LANES, (first + count) * LANES)
-
-    def piece_copies(d, c, into):
-        first, count = PIECES[c]
-        base = lax.div(d * SHARD, LANES)
-        spans = [(base + first, first, count)]
+    for c, (first, count) in enumerate(PIECES):
+
+        def send(k, _, c=c, first=first, count=count):
+            d = lax.rem(me + k, N)
+            src, dst = piece_refs(d, first, count)
+            remote(src, dst, ts.at[c], tr.at[c], d).start()
+            if first + count > TILES:
+                src, dst = last_refs(d)
+                remote(src, dst, ts.at[c], tr.at[c], d).start()
+            return 0
+
+        src, dst = piece_refs(me, first, count)
+        pltpu.make_async_copy(src, dst, tr.at[c]).start()
         if first + count > TILES:
-            spans = [
-                (base + first, first, count - 1),
-                (jnp.minimum(base + TILES, VTILES - 1), TILES, 1),
-            ]
-        for start, at, tiles in spans:
-            yield (
-                teacher.at[:, pl.ds(pl.multiple_of(start * LANES, LANES), tiles * LANES)],
-                into(slice(at * LANES, (at + tiles) * LANES)),
-            )
-
-    for c in range(len(PIECES)):
-        for p, (dy, dz, dc, ry, rz) in enumerate(RELAYED):
-            d = group_index(dy, dz, dc)
-            for src, dst in piece_copies(d, c, lambda cols, p=p: relay.at[p, :, cols]):
-                remote_to(src, dst, ts.at[c], ft.at[c], device(ry, rz, core)).start()
-        for dy, dc in ((1, 0), (3, 0), (1, 1), (3, 1)):
-            d = group_index(dy, 0, dc)
-            for src, dst in piece_copies(d, c, lambda cols: land.at[my_rows, cols]):
-                remote(src, dst, ts.at[c], tr.at[c], d).start()
-        sibling = chip * 2 + (1 - core)
-        for src, dst in piece_copies(sibling, c, lambda cols: land.at[my_rows, cols]):
-            remote(src, dst, ts.at[c], tr.at[c], sibling).start()
-        for src, dst in piece_copies(me, c, lambda cols: land.at[my_rows, cols]):
+            src, dst = last_refs(me)
             pltpu.make_async_copy(src, dst, tr.at[c]).start()
-
-    def forward_pieces(c):
-        cols = columns_of(c)
-        wait_for(relay.at[:, :, cols], ft.at[c])
-        for p, (dy, dz, dc, ry, rz) in enumerate(RELAYED):
-            origin = group_index(4 - ry, 4 - rz, core)
-            rows = pl.ds(pl.multiple_of(origin * ROWS, ROWS), ROWS)
-            remote_to(
-                relay.at[p, :, cols], land.at[rows, cols], fs.at[c], tr.at[c],
-                device(4 + dy - ry, 4 + dz - rz, dc),
-            ).start()
+        lax.fori_loop(1, N, send, 0)
 
     def wait_for(ref, sem):
         pltpu.make_async_copy(ref, ref, sem).wait()
@@ -196,8 +155,6 @@
 
     pltpu.make_async_copy(lse_src, lse_land.at[my_rows, :], mr.at[0]).start()
     lax.fori_loop(1, N, send_lse, 0)
-
-    forward_pieces(0)
 
     local = labels[...] - me * SHARD
     inside = jnp.logical_and(local >= 0, local < SHARD)
@@ -233,61 +190,54 @@
     soft_b[...] = zeros
     hard_b[...] = zeros
     pick_b[...] = zeros
-    for c in range(BLOCKS):
-        w_copies[c].wait()
-
-    forward_pieces(1)
+    for copy in w_copies:
+        copy.wait()
 
     def forward(c):
-        at = pl.ds(pl.multiple_of(c * BLOCK, BLOCK), BLOCK)
-        logits[c] = lax.dot_general(
-            feats[...], w[at, :], (((1,), (1,)), ((), ())), preferred_element_type=F32
+        logits[:, c * FWD : (c + 1) * FWD] = lax.dot_general(
+            feats[...], w[c * FWD : (c + 1) * FWD, :], (((1,), (1,)), ((), ())),
+            preferred_element_type=F32,
         )
 
     def student_sums(c, s):
-        at = pl.ds(s * ROWS, ROWS)
-        tiles = [logits[c, at, i * LANES : (i + 1) * LANES] for i in range(BLOCK_TILES)]
+        at = slice(s * ROWS, (s + 1) * ROWS)
+        tiles = []
+        for i in range(FWD // LANES):
+            start = c * FWD + i * LANES
+            v = logits[at, start : start + LANES]
+            if start + LANES > SHARD:
+                v = jnp.where(lane < SHARD - start, v, -1e30)
+                logits[at, start : start + LANES] = v
+            tiles.append(v)
         top = mx_b[at, :]
-        label = l_b[at, :] - jnp.float32(c * BLOCK)
-        new = jnp.maximum(
-            jnp.maximum(top, tiles[0]), jnp.maximum(jnp.maximum(tiles[1], tiles[2]), tiles[3])
-        )
+        label = l_b[at, :]
+        new = top
+        for v in tiles:
+            new = jnp.maximum(new, v)
         mx_b[at, :] = new
         scale = jnp.exp2((0.5 * LOG2E) * (top - new))
         soft = soft_b[at, :] * scale
         hard = hard_b[at, :] * (scale * scale)
         picked = pick_b[at, :]
         for i, v in enumerate(tiles):
+            if i % BLOCK_TILES == 0:
+                here = label - float(c * FWD + i * LANES)
             e = jnp.exp2((0.5 * LOG2E) * (v - new))
             soft = soft + e
             hard = hard + e * e
-            picked = picked + jnp.where(places[i] == label, v, 0.0)
+            picked = picked + jnp.where(places[i % BLOCK_TILES] == here, v, 0.0)
         soft_b[at, :] = soft
         hard_b[at, :] = hard
         pick_b[at, :] = picked
 
-    forward(0)
-
-    def forward_step(c, _):
-        @pl.when(c == 4)
-        def _():
-            forward_pieces(2)
-
-        for s in range(TOK // ROWS):
-            student_sums(c - 1, s)
-        forward(c)
-        return 0
-
-    lax.fori_loop(1, BLOCKS, forward_step, 0)
-    last = slice((BLOCK_TILES - 1) * LANES, BLOCK)
+    for c in range(FWDS + 1):
+        if c > 0:
+            for s in range(TOK // ROWS):
+                student_sums(c - 1, s)
+        if c < FWDS:
+            forward(c)
+
     wide_lane = lax.broadcasted_iota(jnp.int32, (TOK, LANES), 1)
-    logits[BLOCKS - 1, :, last] = jnp.where(
-        wide_lane < VALID, logits[BLOCKS - 1, :, last], -1e30
-    )
-    for s in range(TOK // ROWS):
-        student_sums(BLOCKS - 1, s)
-    forward_pieces(3)
-
     top = mx_b[...]
     m = jnp.max(top, axis=1, keepdims=True)
     scale = jnp.exp2((0.5 * LOG2E) * (top - m))
@@ -335,8 +285,7 @@
     b_b[...] = jnp.broadcast_to(columns[:, 1:2], (TOK, LANES))
     cross_b[...] = zeros
     inner_b[...] = zeros
-    for n in range(CHIPS):
-        fg[n] = jnp.zeros((TOK, 2 * OWN), F32)
+    fg[...] = jnp.zeros((TOK, D), F32)
     wait_for(lse_land, mr.at[0])
 
     off = lax.rem(me * SHARD, LANES)
@@ -345,11 +294,11 @@
     partner = chip * 2 + (1 - core)
 
     def wait_piece(c):
-        wait_for(land.at[:, columns_of(c)], tr.at[c])
-
-    def gradient(c, s):
+        first, count = PIECES[c]
+        wait_for(land.at[:, first * LANES : (first + count) * LANES], tr.at[c])
+
+    def gradient(c, s, g_v):
         at = pl.ds(s * ROWS, ROWS)
-        slot = lax.rem(c, 2)
         lse_s, b, ct = a_b[at, :], b_b[at, :], c_b[at, :]
         label = l_b[at, :] - jnp.float32(c * BLOCK)
         lse_t = lse_land[at, :]
@@ -365,7 +314,7 @@
             after = turned(i + 1)
             x = jnp.where(keep, here, after)
             here = after
-            v = logits[c, at, i * LANES : (i + 1) * LANES]
+            v = logits[at, pl.ds(pl.multiple_of(c * BLOCK + i * LANES, LANES), LANES)]
             p = jnp.exp2((0.5 * LOG2E) * x - lse_t)
             e = jnp.exp2((0.5 * LOG2E) * v - lse_s)
             if i == BLOCK_TILES - 1:
@@ -374,20 +323,14 @@
             g = e * (ct + e * b) - ct * p
             g = g - jnp.where(places[i] == label, half, 0.0)
             g = g.astype(BF16)
-            g_v[slot, at, i * LANES : (i + 1) * LANES] = g
+            g_v[at, i * LANES : (i + 1) * LANES] = g
             inner = inner + g.astype(F32) * v
         cross_b[at, :] = cross
         inner_b[at, :] = inner
 
-    def backward(c, n):
-        rows = pl.ds(pl.multiple_of(c * BLOCK, BLOCK), BLOCK)
-        at = pl.ds(pl.multiple_of(n * (2 * OWN), 2 * OWN), 2 * OWN)
-        part = jnp.dot(g_v[lax.rem(c, 2)], w[rows, at], preferred_element_type=F32)
-        return fg[n] + part
-
     wait_piece(0)
     for s in range(TOK // ROWS):
-        gradient(0, s)
+        gradient(0, s, g_now)
 
     def step(c, _):
         for p in range(1, len(PIECES)):
@@ -397,9 +340,10 @@
                 wait_piece(p)
 
         for s in range(TOK // ROWS):
-            gradient(c + 1, s)
-        for n in range(CHIPS):
-            fg[n] = backward(c, n)
+            gradient(c + 1, s, g_next)
+        rows = pl.ds(pl.multiple_of(c * BLOCK, BLOCK), BLOCK)
+        fg[...] += jnp.dot(g_now[...], w[rows, :], preferred_element_type=F32)
+        g_now[...] = g_next[...]
         return 0
 
     lax.fori_loop(0, BLOCKS - 1, step, 0)
@@ -418,18 +362,21 @@
     pltpu.make_async_copy(fin_src, fin_land.at[me], mr.at[2]).start()
     lax.fori_loop(1, N, send_final, 0)
 
-    for k in range(CHIPS):
+    fg[...] += jnp.dot(g_now[...], w[PAD - BLOCK :, :], preferred_element_type=F32)
+
+    def half_of(n, c):
+        return fg[:, pl.ds(pl.multiple_of((2 * n + c) * OWN, OWN), OWN)]
+
+    def give(k, _):
         n = lax.rem(chip + 1 + k, CHIPS)
-        part = backward(BLOCKS - 1, n)
-        fg[n] = part
-        theirs = jnp.where(core == 0, part[:, OWN:], part[:, :OWN])
-        cx_src[n] = theirs.astype(BF16)
+        cx_src[n] = half_of(n, 1 - core).astype(BF16)
         remote(cx_src.at[n], cx_land.at[n], cs.at[0], cr.at[n], partner).start()
+        return 0
+
+    lax.fori_loop(0, CHIPS, give, 0)
 
     def own_half(n):
-        part = fg[n]
-        half = jnp.where(core == 0, part[:, :OWN], part[:, OWN:])
-        return half + cx_land[n].astype(F32)
+        return half_of(n, core) + cx_land[n].astype(F32)
 
     def share(k, _):
         n = lax.rem(chip + 1 + k, CHIPS)
@@ -440,7 +387,6 @@
 
     lax.fori_loop(0, CHIPS - 1, share, 0)
     wait_for(cx_land.at[chip], cr.at[chip])
-    fg[chip, :, :OWN] = own_half(chip)
 
     wait_for(fin_land, mr.at[2])
     cross = jnp.zeros((1, TOK), F32)
@@ -458,16 +404,15 @@
 
     wait_for(rs_land.at[0 : CHIPS - 1], rr)
     mine = pl.ds(pl.multiple_of(me * OWN, OWN), OWN)
-    total = fg[chip, :, :OWN]
+    total = own_half(chip)
     for k in range(1, CHIPS):
         total = total + rs_land[lax.rem(chip + k, CHIPS)].astype(F32)
     r = r_b[...]
     normed = hid[:, mine].astype(F32) * r
     out[...] = (r * (gain[:, mine] * total - normed * a_b[...])).astype(BF16)
 
-    for c in range(len(PIECES)):
-        wait_for(land.at[0 : TOK - ROWS, columns_of(c)], ts.at[c])
-        wait_for(relay.at[:, :, columns_of(c)], fs.at[c])
+    for c, (first, count) in enumerate(PIECES):
+        wait_for(land.at[0 : TOK - ROWS, first * LANES : (first + count) * LANES], ts.at[c])
     wait_for(lse_land.at[0 : TOK - ROWS], ms.at[0])
     wait_for(st_land.at[0 : N - 1], ms.at[1])
     wait_for(fin_land.at[0 : N - 1], ms.at[2])
@@ -493,11 +438,11 @@
             pltpu.VMEM((PAD, D), BF16),
             pltpu.VMEM((ROWS, VOCAB), BF16),
             pltpu.VMEM((TOK, PAD + LANES), BF16),
-            pltpu.VMEM((len(RELAYED), ROWS, PAD + LANES), BF16),
             pltpu.VMEM((TOK, D), BF16),
-            pltpu.VMEM((BLOCKS, TOK, BLOCK), F32),
-            pltpu.VMEM((CHIPS, TOK, 2 * OWN), F32),
-            pltpu.VMEM((2, TOK, BLOCK), BF16),
+            pltpu.VMEM((TOK, PAD), F32),
+            pltpu.VMEM((TOK, D), F32),
+            pltpu.VMEM((TOK, BLOCK), BF16),
+            pltpu.VMEM((TOK, BLOCK), BF16),
             pltpu.VMEM((ROWS, LANES), F32),
             column,
             pltpu.VMEM((8, TOK), F32),
@@ -511,7 +456,7 @@
             column, column, column, column, column, column,
             column, column, column, column, column,
             pltpu.VMEM((8, TOK), F32),
-            dma((2,)), dma((BLOCKS,)), dma((len(PIECES),)), dma((len(PIECES),)), dma((len(PIECES),)), dma((len(PIECES),)),
+            dma((2,)), dma((BLOCKS,)), dma((len(PIECES),)), dma((len(PIECES),)),
             dma((3,)), dma((3,)), dma((1,)), dma((CHIPS,)), dma, dma,
         ],
         compiler_params=pltpu.CompilerParams(

time: 63 us -> 62.1 us (0.986)
  Pallas kernels: 59.5 us -> 58.6 us
    pallas_call x1, Pallas kernels: 59.5 us -> 58.6 us  [on_device(): pl.pallas_call(kernel, out_shape=(jax.ShapeDtypeStruct((TOK, OWN), BF16),...]
where the time goes in v2:
time: 62.1 us; the launch traced here: 61.9 us
  Pallas kernels  58.6 us (94%)
  local copies, waits for them, and re-layouts  2.67 us (4%)
  between operations  0.64 us (1%)
    pallas_call x1, Pallas kernels, on_device(): pl.pallas_call(kernel, out_shape=(jax.ShapeDtypeStruct((TOK, OWN), BF16),...  58.6 us
    unnamed x2, local copies, waits for them, and re-layouts  2.67 us

profile of v2, /device:TPU:1, one launch (start us, length us, event | category | flops | bytes accessed | tf_op | source)
XLA Modules:
  0.0 61.9 jit_solution(1806398922709499677)
XLA Ops:
  0.6 58.6 %shard_map.77 = (bf16[256,128]{1,0:T(8,128)(2,1)}, f32[1,256]{1,0:T(1,128)}) custom-call(bf16[256,2048]{1,0:T(8,128)(2,1)} %hidden.1, f32[1,2048]{1,0:T(1,128)} %bitcast.7, bf16[4008,2048]{1,0:T(8,128)(2,1)} %bitcast.6, bf16[16,64128]{1,0:T(8,128)(2,1)} %teacher.1, s32[1,256]{1,0:T(1,128)} %bitcast.8, f32[1,256]{1,0:T(1,128)} %bitcast.9), custom_call_target="tpu_custom_call" | custom-call | flops 8405385216 | bytes 20000000 | tf_op jit(solution)/shard_map/pallas_call | solution.py:428
  59.2 1.5 %copy.10 = bf16[256,128]{1,0:T(8,128)(2,1)} copy(bf16[256,128]{1,0:T(8,128)(2,1)} %get-tuple-element.8) | data formatting | bytes 131072
  60.7 1.2 %copy.11 = f32[256]{0:T(256)} copy(f32[256]{0:T(256)} %bitcast.5) | data formatting | bytes 2048

commit v3 on v1

--- a/solution.py
+++ b/solution.py
@@ -25,6 +25,8 @@
 BLOCK = 512
 BLOCKS = PAD // BLOCK
 BLOCK_TILES = BLOCK // LANES
+FWD = 1024
+FWDS = PAD // FWD
 LOG2E = 1.4426950408889634
 LN2 = 0.6931471805599453
 RELAYED = (
@@ -42,7 +44,7 @@
 def kernel(
     hidden, gain, wt, teacher, labels, cot,
     out, loss,
-    hid, w, t_v, land, relay, feats, logits, fg, g_v,
+    hid, w, t_v, land, relay, feats, logits, fg, g_now, g_next,
     lse_src, lse_land, st_src, st_land, fin_src, fin_land,
     cx_src, cx_land, rs_src, rs_land,
     a_b, b_b, c_b, l_b, r_b, mx_b, soft_b, hard_b, pick_b, cross_b, inner_b, rows_v,
@@ -233,61 +235,59 @@
     soft_b[...] = zeros
     hard_b[...] = zeros
     pick_b[...] = zeros
-    for c in range(BLOCKS):
-        w_copies[c].wait()
+    for copy in w_copies:
+        copy.wait()
 
     forward_pieces(1)
 
     def forward(c):
-        at = pl.ds(pl.multiple_of(c * BLOCK, BLOCK), BLOCK)
-        logits[c] = lax.dot_general(
-            feats[...], w[at, :], (((1,), (1,)), ((), ())), preferred_element_type=F32
+        logits[:, c * FWD : (c + 1) * FWD] = lax.dot_general(
+            feats[...], w[c * FWD : (c + 1) * FWD, :], (((1,), (1,)), ((), ())),
+            preferred_element_type=F32,
         )
 
     def student_sums(c, s):
-        at = pl.ds(s * ROWS, ROWS)
-        tiles = [logits[c, at, i * LANES : (i + 1) * LANES] for i in range(BLOCK_TILES)]
+        at = slice(s * ROWS, (s + 1) * ROWS)
+        tiles = []
+        for i in range(FWD // LANES):
+            start = c * FWD + i * LANES
+            v = logits[at, start : start + LANES]
+            if start + LANES > SHARD:
+                v = jnp.where(lane < SHARD - start, v, -1e30)
+                logits[at, start : start + LANES] = v
+            tiles.append(v)
         top = mx_b[at, :]
-        label = l_b[at, :] - jnp.float32(c * BLOCK)
-        new = jnp.maximum(
-            jnp.maximum(top, tiles[0]), jnp.maximum(jnp.maximum(tiles[1], tiles[2]), tiles[3])
-        )
+        label = l_b[at, :]
+        new = top
+        for v in tiles:
+            new = jnp.maximum(new, v)
         mx_b[at, :] = new
         scale = jnp.exp2((0.5 * LOG2E) * (top - new))
         soft = soft_b[at, :] * scale
         hard = hard_b[at, :] * (scale * scale)
         picked = pick_b[at, :]
         for i, v in enumerate(tiles):
+            if i % BLOCK_TILES == 0:
+                here = label - float(c * FWD + i * LANES)
             e = jnp.exp2((0.5 * LOG2E) * (v - new))
             soft = soft + e
             hard = hard + e * e
-            picked = picked + jnp.where(places[i] == label, v, 0.0)
+            picked = picked + jnp.where(places[i % BLOCK_TILES] == here, v, 0.0)
         soft_b[at, :] = soft
         hard_b[at, :] = hard
         pick_b[at, :] = picked
 
-    forward(0)
-
-    def forward_step(c, _):
-        @pl.when(c == 4)
-        def _():
+    for c in range(FWDS + 1):
+        if c == 2:
             forward_pieces(2)
-
-        for s in range(TOK // ROWS):
-            student_sums(c - 1, s)
-        forward(c)
-        return 0
-
-    lax.fori_loop(1, BLOCKS, forward_step, 0)
-    last = slice((BLOCK_TILES - 1) * LANES, BLOCK)
+        if c > 0:
+            for s in range(TOK // ROWS):
+                student_sums(c - 1, s)
+        if c < FWDS:
+            forward(c)
+
+    forward_pieces(3)
     wide_lane = lax.broadcasted_iota(jnp.int32, (TOK, LANES), 1)
-    logits[BLOCKS - 1, :, last] = jnp.where(
-        wide_lane < VALID, logits[BLOCKS - 1, :, last], -1e30
-    )
-    for s in range(TOK // ROWS):
-        student_sums(BLOCKS - 1, s)
-    forward_pieces(3)
-
     top = mx_b[...]
     m = jnp.max(top, axis=1, keepdims=True)
     scale = jnp.exp2((0.5 * LOG2E) * (top - m))
@@ -335,8 +335,7 @@
     b_b[...] = jnp.broadcast_to(columns[:, 1:2], (TOK, LANES))
     cross_b[...] = zeros
     inner_b[...] = zeros
-    for n in range(CHIPS):
-        fg[n] = jnp.zeros((TOK, 2 * OWN), F32)
+    fg[...] = jnp.zeros((TOK, D), F32)
     wait_for(lse_land, mr.at[0])
 
     off = lax.rem(me * SHARD, LANES)
@@ -347,9 +346,8 @@
     def wait_piece(c):
         wait_for(land.at[:, columns_of(c)], tr.at[c])
 
-    def gradient(c, s):
+    def gradient(c, s, g_v):
         at = pl.ds(s * ROWS, ROWS)
-        slot = lax.rem(c, 2)
         lse_s, b, ct = a_b[at, :], b_b[at, :], c_b[at, :]
         label = l_b[at, :] - jnp.float32(c * BLOCK)
         lse_t = lse_land[at, :]
@@ -365,7 +363,7 @@
             after = turned(i + 1)
             x = jnp.where(keep, here, after)
             here = after
-            v = logits[c, at, i * LANES : (i + 1) * LANES]
+            v = logits[at, pl.ds(pl.multiple_of(c * BLOCK + i * LANES, LANES), LANES)]
             p = jnp.exp2((0.5 * LOG2E) * x - lse_t)
             e = jnp.exp2((0.5 * LOG2E) * v - lse_s)
             if i == BLOCK_TILES - 1:
@@ -374,20 +372,14 @@
             g = e * (ct + e * b) - ct * p
             g = g - jnp.where(places[i] == label, half, 0.0)
             g = g.astype(BF16)
-            g_v[slot, at, i * LANES : (i + 1) * LANES] = g
+            g_v[at, i * LANES : (i + 1) * LANES] = g
             inner = inner + g.astype(F32) * v
         cross_b[at, :] = cross
         inner_b[at, :] = inner
 
-    def backward(c, n):
-        rows = pl.ds(pl.multiple_of(c * BLOCK, BLOCK), BLOCK)
-        at = pl.ds(pl.multiple_of(n * (2 * OWN), 2 * OWN), 2 * OWN)
-        part = jnp.dot(g_v[lax.rem(c, 2)], w[rows, at], preferred_element_type=F32)
-        return fg[n] + part
-
     wait_piece(0)
     for s in range(TOK // ROWS):
-        gradient(0, s)
+        gradient(0, s, g_now)
 
     def step(c, _):
         for p in range(1, len(PIECES)):
@@ -397,9 +389,10 @@
                 wait_piece(p)
 
         for s in range(TOK // ROWS):
-            gradient(c + 1, s)
-        for n in range(CHIPS):
-            fg[n] = backward(c, n)
+            gradient(c + 1, s, g_next)
+        rows = pl.ds(pl.multiple_of(c * BLOCK, BLOCK), BLOCK)
+        fg[...] += jnp.dot(g_now[...], w[rows, :], preferred_element_type=F32)
+        g_now[...] = g_next[...]
         return 0
 
     lax.fori_loop(0, BLOCKS - 1, step, 0)
@@ -418,18 +411,21 @@
     pltpu.make_async_copy(fin_src, fin_land.at[me], mr.at[2]).start()
     lax.fori_loop(1, N, send_final, 0)
 
-    for k in range(CHIPS):
+    fg[...] += jnp.dot(g_now[...], w[PAD - BLOCK :, :], preferred_element_type=F32)
+
+    def half_of(n, c):
+        return fg[:, pl.ds(pl.multiple_of((2 * n + c) * OWN, OWN), OWN)]
+
+    def give(k, _):
         n = lax.rem(chip + 1 + k, CHIPS)
-        part = backward(BLOCKS - 1, n)
-        fg[n] = part
-        theirs = jnp.where(core == 0, part[:, OWN:], part[:, :OWN])
-        cx_src[n] = theirs.astype(BF16)
+        cx_src[n] = half_of(n, 1 - core).astype(BF16)
         remote(cx_src.at[n], cx_land.at[n], cs.at[0], cr.at[n], partner).start()
+        return 0
+
+    lax.fori_loop(0, CHIPS, give, 0)
 
     def own_half(n):
-        part = fg[n]
-        half = jnp.where(core == 0, part[:, :OWN], part[:, OWN:])
-        return half + cx_land[n].astype(F32)
+        return half_of(n, core) + cx_land[n].astype(F32)
 
     def share(k, _):
         n = lax.rem(chip + 1 + k, CHIPS)
@@ -440,7 +436,6 @@
 
     lax.fori_loop(0, CHIPS - 1, share, 0)
     wait_for(cx_land.at[chip], cr.at[chip])
-    fg[chip, :, :OWN] = own_half(chip)
 
     wait_for(fin_land, mr.at[2])
     cross = jnp.zeros((1, TOK), F32)
@@ -458,7 +453,7 @@
 
     wait_for(rs_land.at[0 : CHIPS - 1], rr)
     mine = pl.ds(pl.multiple_of(me * OWN, OWN), OWN)
-    total = fg[chip, :, :OWN]
+    total = own_half(chip)
     for k in range(1, CHIPS):
         total = total + rs_land[lax.rem(chip + k, CHIPS)].astype(F32)
     r = r_b[...]
@@ -495,9 +490,10 @@
             pltpu.VMEM((TOK, PAD + LANES), BF16),
             pltpu.VMEM((len(RELAYED), ROWS, PAD + LANES), BF16),
             pltpu.VMEM((TOK, D), BF16),
-            pltpu.VMEM((BLOCKS, TOK, BLOCK), F32),
-            pltpu.VMEM((CHIPS, TOK, 2 * OWN), F32),
-            pltpu.VMEM((2, TOK, BLOCK), BF16),
+            pltpu.VMEM((TOK, PAD), F32),
+            pltpu.VMEM((TOK, D), F32),
+            pltpu.VMEM((TOK, BLOCK), BF16),
+            pltpu.VMEM((TOK, BLOCK), BF16),
             pltpu.VMEM((ROWS, LANES), F32),
             column,
             pltpu.VMEM((8, TOK), F32),

time: 63 us -> 62.2 us (0.987)
  Pallas kernels: 59.5 us -> 58.6 us
    pallas_call x1, Pallas kernels: 59.5 us -> 58.6 us  [on_device(): pl.pallas_call(kernel, out_shape=(jax.ShapeDtypeStruct((TOK, OWN), BF16),...]
where the time goes in v3:
time: 62.2 us; the launch traced here: 61.9 us
  Pallas kernels  58.6 us (94%)
  local copies, waits for them, and re-layouts  2.67 us (4%)
  between operations  0.64 us (1%)
    pallas_call x1, Pallas kernels, on_device(): pl.pallas_call(kernel, out_shape=(jax.ShapeDtypeStruct((TOK, OWN), BF16),...  58.6 us
    unnamed x2, local copies, waits for them, and re-layouts  2.67 us

profile of v3, /device:TPU:1, one launch (start us, length us, event | category | flops | bytes accessed | tf_op | source)
XLA Modules:
  0.0 61.9 jit_solution(7017651280213963133)
XLA Ops:
  0.6 58.6 %shard_map.77 = (bf16[256,128]{1,0:T(8,128)(2,1)}, f32[1,256]{1,0:T(1,128)}) custom-call(bf16[256,2048]{1,0:T(8,128)(2,1)} %hidden.1, f32[1,2048]{1,0:T(1,128)} %bitcast.7, bf16[4008,2048]{1,0:T(8,128)(2,1)} %bitcast.6, bf16[16,64128]{1,0:T(8,128)(2,1)} %teacher.1, s32[1,256]{1,0:T(1,128)} %bitcast.8, f32[1,256]{1,0:T(1,128)} %bitcast.9), custom_call_target="tpu_custom_call" | custom-call | flops 8405385216 | bytes 20000000 | tf_op jit(solution)/shard_map/pallas_call | solution.py:478
  59.3 1.5 %copy.10 = bf16[256,128]{1,0:T(8,128)(2,1)} copy(bf16[256,128]{1,0:T(8,128)(2,1)} %get-tuple-element.8) | data formatting | bytes 131072
  60.7 1.2 %copy.11 = f32[256]{0:T(256)} copy(f32[256]{0:T(256)} %bitcast.5) | data formatting | bytes 2048

commit v4 on v2

--- a/solution.py
+++ b/solution.py
@@ -46,6 +46,8 @@
     me = lax.axis_index("vocab")
     chip = lax.div(me, 2)
     core = lax.rem(me, 2)
+    y = lax.rem(chip, 4)
+    z_hi = lax.div(me, 8)
     lane = lax.broadcasted_iota(jnp.int32, (ROWS, LANES), 1)
     places = [(lane + i * LANES).astype(F32) for i in range(BLOCK_TILES)]
     my_rows = pl.ds(pl.multiple_of(me * ROWS, ROWS), ROWS)
@@ -58,9 +60,9 @@
     w_copies = []
     for c in range(BLOCKS):
         lo, hi = c * BLOCK, min((c + 1) * BLOCK, SHARD)
-        copy = pltpu.make_async_copy(wt.at[lo:hi], w.at[lo:hi], w_sem.at[c])
+        w_copies.append(pltpu.make_async_copy(wt.at[lo:hi], w.at[lo:hi], w_sem.at[c]))
+    for copy in w_copies[:2]:
         copy.start()
-        w_copies.append(copy)
 
     barrier = pltpu.get_barrier_semaphore()
 
@@ -72,20 +74,6 @@
 
     lax.fori_loop(1, N, greet, 0)
     pl.semaphore_wait(barrier, N - 1)
-
-    def piece_refs(d, first, count):
-        base = lax.div(d * SHARD, LANES) + first
-        if first + count > TILES:
-            count = count - 1
-        src = teacher.at[:, pl.ds(pl.multiple_of(base * LANES, LANES), count * LANES)]
-        dst = land.at[my_rows, first * LANES : (first + count) * LANES]
-        return src, dst
-
-    def last_refs(d):
-        base = jnp.minimum(lax.div(d * SHARD, LANES) + TILES, VTILES - 1)
-        src = teacher.at[:, pl.ds(pl.multiple_of(base * LANES, LANES), LANES)]
-        dst = land.at[my_rows, TILES * LANES : (TILES + 1) * LANES]
-        return src, dst
 
     def remote(src, dst, send_sem, recv_sem, d):
         return pltpu.make_async_remote_copy(
@@ -93,23 +81,34 @@
             device_id={"vocab": d}, device_id_type=MESH,
         )
 
-    for c, (first, count) in enumerate(PIECES):
-
-        def send(k, _, c=c, first=first, count=count):
-            d = lax.rem(me + k, N)
-            src, dst = piece_refs(d, first, count)
-            remote(src, dst, ts.at[c], tr.at[c], d).start()
-            if first + count > TILES:
-                src, dst = last_refs(d)
-                remote(src, dst, ts.at[c], tr.at[c], d).start()
-            return 0
-
-        src, dst = piece_refs(me, first, count)
-        pltpu.make_async_copy(src, dst, tr.at[c]).start()
+    def piece_copies(d, c):
+        first, count = PIECES[c]
+        base = lax.div(d * SHARD, LANES)
+        spans = [(base + first, first, count)]
         if first + count > TILES:
-            src, dst = last_refs(me)
+            spans = [
+                (base + first, first, count - 1),
+                (jnp.minimum(base + TILES, VTILES - 1), TILES, 1),
+            ]
+        for start, at, tiles in spans:
+            yield (
+                teacher.at[:, pl.ds(pl.multiple_of(start * LANES, LANES), tiles * LANES)],
+                land.at[my_rows, at * LANES : (at + tiles) * LANES],
+            )
+
+    for c in range(len(PIECES)):
+        for dc in (0, 1):
+            for dy, dz in ((0, 1), (1, 0), (3, 0), (2, 1), (1, 1), (2, 0), (3, 1)):
+                d = (lax.rem(z_hi + dz, 2) * 4 + lax.rem(y + dy, 4)) * 2 + lax.rem(core + dc, 2)
+                for src, dst in piece_copies(d, c):
+                    remote(src, dst, ts.at[c], tr.at[c], d).start()
+        sibling = chip * 2 + (1 - core)
+        for src, dst in piece_copies(sibling, c):
+            remote(src, dst, ts.at[c], tr.at[c], sibling).start()
+        for src, dst in piece_copies(me, c):
             pltpu.make_async_copy(src, dst, tr.at[c]).start()
-        lax.fori_loop(1, N, send, 0)
+        for copy in w_copies[2 + 2 * c : 4 + 2 * c]:
+            copy.start()
 
     def wait_for(ref, sem):
         pltpu.make_async_copy(ref, ref, sem).wait()
@@ -190,10 +189,10 @@
     soft_b[...] = zeros
     hard_b[...] = zeros
     pick_b[...] = zeros
-    for copy in w_copies:
-        copy.wait()
 
     def forward(c):
+        for copy in w_copies[c * FWD // BLOCK : (c + 1) * FWD // BLOCK]:
+            copy.wait()
         logits[:, c * FWD : (c + 1) * FWD] = lax.dot_general(
             feats[...], w[c * FWD : (c + 1) * FWD, :], (((1,), (1,)), ((), ())),
             preferred_element_type=F32,
@@ -418,6 +417,11 @@
     wait_for(fin_land.at[0 : N - 1], ms.at[2])
     wait_for(cx_src, cs.at[0])
     wait_for(rs_src.at[0 : CHIPS - 1], rs)
+
+
+def finish(grad, loss, grad_out, loss_out):
+    grad_out[...] = grad[...]
+    loss_out[...] = loss[...]
 
 
 def on_device(hidden, norm_gain, head_weight, teacher, labels, cotangent):
@@ -473,6 +477,15 @@
         labels.reshape(1, TOK),
         cotangent.reshape(1, TOK),
     )
+    grad, loss = pl.pallas_call(
+        finish,
+        out_shape=(
+            jax.ShapeDtypeStruct((TOK, OWN), BF16),
+            jax.ShapeDtypeStruct((1, TOK), F32),
+        ),
+        in_specs=[vmem, vmem],
+        out_specs=(vmem, vmem),
+    )(grad, loss)
     return grad, loss.reshape(TOK)
 
 

time: 62.1 us -> 60.8 us (0.979)
  local copies, waits for them, and re-layouts: 2.67 us -> 0 us
  Pallas kernels: 58.6 us -> 59.9 us
    unnamed x2 -> x0, local copies, waits for them, and re-layouts: 2.67 us -> none
    pallas_call x0 -> x1, Pallas kernels: none -> 1.48 us  [on_device(): pl.pallas_call(finish, out_shape=(jax.ShapeDtypeStruct((TOK, OWN), BF16),...]
where the time goes in v4:
time: 60.8 us; the launch traced here: 60.6 us
  Pallas kernels  59.9 us (99%)
  between operations  0.64 us (1%)
    pallas_call x1, Pallas kernels, on_device(): pl.pallas_call(kernel, out_shape=(jax.ShapeDtypeStruct((TOK, OWN), BF16),...  58.5 us
    pallas_call x1, Pallas kernels, on_device(): pl.pallas_call(finish, out_shape=(jax.ShapeDtypeStruct((TOK, OWN), BF16),...  1.48 us

profile of v4, /device:TPU:1, one launch (start us, length us, event | category | flops | bytes accessed | tf_op | source)
XLA Modules:
  0.0 60.6 jit_solution(1396232119662620817)
XLA Ops:
  0.6 58.5 %shard_map.77 = (bf16[256,128]{1,0:T(8,128)(2,1)}, f32[1,256]{1,0:T(1,128)}) custom-call(bf16[256,2048]{1,0:T(8,128)(2,1)} %hidden.1, f32[1,2048]{1,0:T(1,128)} %bitcast.6, bf16[4008,2048]{1,0:T(8,128)(2,1)} %bitcast.5, bf16[16,64128]{1,0:T(8,128)(2,1)} %teacher.1, s32[1,256]{1,0:T(1,128)} %bitcast.7, f32[1,256]{1,0:T(1,128)} %bitcast.8), custom_call_target="tpu_custom_call" | custom-call | flops 8405385216 | bytes 20000000 | tf_op jit(solution)/shard_map/pallas_call | solution.py:432
  59.1 1.5 %shard_map.78 = (bf16[256,128]{1,0:T(8,128)(2,1)}, f32[1,256]{1,0:T(1,128)}) custom-call(bf16[256,128]{1,0:T(8,128)(2,1)} %get-tuple-element.6.grad, f32[1,256]{1,0:T(1,128)} %get-tuple-element.7.loss), custom_call_target="tpu_custom_call" | custom-call | tf_op jit(solution)/shard_map/pallas_call | solution.py:480

commit v5 on v4

--- a/solution.py
+++ b/solution.py
@@ -96,7 +96,7 @@
                 land.at[my_rows, at * LANES : (at + tiles) * LANES],
             )
 
-    for c in range(len(PIECES)):
+    def send_piece(c):
         for dc in (0, 1):
             for dy, dz in ((0, 1), (1, 0), (3, 0), (2, 1), (1, 1), (2, 0), (3, 1)):
                 d = (lax.rem(z_hi + dz, 2) * 4 + lax.rem(y + dy, 4)) * 2 + lax.rem(core + dc, 2)
@@ -107,8 +107,10 @@
             remote(src, dst, ts.at[c], tr.at[c], sibling).start()
         for src, dst in piece_copies(me, c):
             pltpu.make_async_copy(src, dst, tr.at[c]).start()
-        for copy in w_copies[2 + 2 * c : 4 + 2 * c]:
-            copy.start()
+
+    send_piece(0)
+    for copy in w_copies[2:]:
+        copy.start()
 
     def wait_for(ref, sem):
         pltpu.make_async_copy(ref, ref, sem).wait()
@@ -154,6 +156,8 @@
 
     pltpu.make_async_copy(lse_src, lse_land.at[my_rows, :], mr.at[0]).start()
     lax.fori_loop(1, N, send_lse, 0)
+
+    send_piece(1)
 
     local = labels[...] - me * SHARD
     inside = jnp.logical_and(local >= 0, local < SHARD)
@@ -254,6 +258,8 @@
 
     pltpu.make_async_copy(st_src, st_land.at[me], mr.at[1]).start()
     lax.fori_loop(1, N, send_stats, 0)
+    send_piece(2)
+    send_piece(3)
     wait_for(st_land, mr.at[1])
 
     top = st_land[0, 0:1, :]

time: 60.8 us -> 53.5 us (0.88)
  Pallas kernels: 59.9 us -> 52.7 us
    pallas_call x1, Pallas kernels: 58.5 us -> 51.2 us  [on_device(): pl.pallas_call(kernel, out_shape=(jax.ShapeDtypeStruct((TOK, OWN), BF16),...]
where the time goes in v5:
time: 53.5 us; the launch traced here: 53.3 us
  Pallas kernels  52.7 us (99%)
  between operations  0.64 us (1%)
    pallas_call x1, Pallas kernels, on_device(): pl.pallas_call(kernel, out_shape=(jax.ShapeDtypeStruct((TOK, OWN), BF16),...  51.2 us
    pallas_call x1, Pallas kernels, on_device(): pl.pallas_call(finish, out_shape=(jax.ShapeDtypeStruct((TOK, OWN), BF16),...  1.48 us

profile of v5, /device:TPU:1, one launch (start us, length us, event | category | flops | bytes accessed | tf_op | source)
XLA Modules:
  0.0 53.3 jit_solution(8462429674495261605)
XLA Ops:
  0.6 51.2 %shard_map.77 = (bf16[256,128]{1,0:T(8,128)(2,1)}, f32[1,256]{1,0:T(1,128)}) custom-call(bf16[256,2048]{1,0:T(8,128)(2,1)} %hidden.1, f32[1,2048]{1,0:T(1,128)} %bitcast.6, bf16[4008,2048]{1,0:T(8,128)(2,1)} %bitcast.5, bf16[16,64128]{1,0:T(8,128)(2,1)} %teacher.1, s32[1,256]{1,0:T(1,128)} %bitcast.7, f32[1,256]{1,0:T(1,128)} %bitcast.8), custom_call_target="tpu_custom_call" | custom-call | flops 8405385216 | bytes 20000000 | tf_op jit(solution)/shard_map/pallas_call | solution.py:438
  51.9 1.5 %shard_map.78 = (bf16[256,128]{1,0:T(8,128)(2,1)}, f32[1,256]{1,0:T(1,128)}) custom-call(bf16[256,128]{1,0:T(8,128)(2,1)} %get-tuple-element.6.grad, f32[1,256]{1,0:T(1,128)} %get-tuple-element.7.loss), custom_call_target="tpu_custom_call" | custom-call | tf_op jit(solution)/shard_map/pallas_call | solution.py:486

commit v6 on v5

--- a/solution.py
+++ b/solution.py
@@ -21,7 +21,8 @@
 PAD = TILES * LANES
 VTILES = VOCAB // LANES
 VALID = SHARD - (TILES - 1) * LANES
-PIECES = ((0, 9), (9, 8), (17, 8), (25, 8))
+PIECES = ((0, 9), (9, 8), (17, 8), (25, 4), (29, 4))
+FIRST_BLOCK = (0, 2, 4, 6, 7)
 BLOCK = 512
 BLOCKS = PAD // BLOCK
 BLOCK_TILES = BLOCK // LANES
@@ -234,6 +235,8 @@
         pick_b[at, :] = picked
 
     for c in range(FWDS + 1):
+        if c == 2:
+            send_piece(2)
         if c > 0:
             for s in range(TOK // ROWS):
                 student_sums(c - 1, s)
@@ -258,8 +261,8 @@
 
     pltpu.make_async_copy(st_src, st_land.at[me], mr.at[1]).start()
     lax.fori_loop(1, N, send_stats, 0)
-    send_piece(2)
     send_piece(3)
+    send_piece(4)
     wait_for(st_land, mr.at[1])
 
     top = st_land[0, 0:1, :]
@@ -340,7 +343,7 @@
     def step(c, _):
         for p in range(1, len(PIECES)):
 
-            @pl.when(c + 1 == 2 * p)
+            @pl.when(c + 1 == FIRST_BLOCK[p])
             def _():
                 wait_piece(p)
 
@@ -353,6 +356,18 @@
 
     lax.fori_loop(0, BLOCKS - 1, step, 0)
 
+    def half_of(n, c):
+        return fg[:, pl.ds(pl.multiple_of((2 * n + c) * OWN, OWN), OWN)]
+
+    for h in range(2):
+        cols = slice(h * (D // 2), (h + 1) * (D // 2))
+        fg[:, cols] += jnp.dot(
+            g_now[...], w[PAD - BLOCK :, cols], preferred_element_type=F32
+        )
+        for n in range(h * CHIPS // 2, (h + 1) * CHIPS // 2):
+            cx_src[n] = half_of(n, 1 - core).astype(BF16)
+            remote(cx_src.at[n], cx_land.at[n], cs.at[0], cr.at[n], partner).start()
+
     cross = jnp.sum(cross_b[...], axis=1, keepdims=True)
     inner = jnp.sum(inner_b[...], axis=1, keepdims=True)
     stat = jnp.where(wide_lane == 0, cross, inner)
@@ -366,19 +381,6 @@
 
     pltpu.make_async_copy(fin_src, fin_land.at[me], mr.at[2]).start()
     lax.fori_loop(1, N, send_final, 0)
-
-    fg[...] += jnp.dot(g_now[...], w[PAD - BLOCK :, :], preferred_element_type=F32)
-
-    def half_of(n, c):
-        return fg[:, pl.ds(pl.multiple_of((2 * n + c) * OWN, OWN), OWN)]
-
-    def give(k, _):
-        n = lax.rem(chip + 1 + k, CHIPS)
-        cx_src[n] = half_of(n, 1 - core).astype(BF16)
-        remote(cx_src.at[n], cx_land.at[n], cs.at[0], cr.at[n], partner).start()
-        return 0
-
-    lax.fori_loop(0, CHIPS, give, 0)
 
     def own_half(n):
         return half_of(n, core) + cx_land[n].astype(F32)

time: 53.5 us -> 55.2 us (1.032)
  Pallas kernels: 52.7 us -> 54.2 us
    pallas_call x1, Pallas kernels: 51.2 us -> 52.8 us  [on_device(): pl.pallas_call(kernel, out_shape=(jax.ShapeDtypeStruct((TOK, OWN), BF16),...]
where the time goes in v6:
time: 55.2 us; the launch traced here: 54.9 us
  Pallas kernels  54.2 us (98%)
  between operations  0.64 us (1%)
    pallas_call x1, Pallas kernels, on_device(): pl.pallas_call(kernel, out_shape=(jax.ShapeDtypeStruct((TOK, OWN), BF16),...  52.8 us
    pallas_call x1, Pallas kernels, on_device(): pl.pallas_call(finish, out_shape=(jax.ShapeDtypeStruct((TOK, OWN), BF16),...  1.48 us

profile of v6, /device:TPU:1, one launch (start us, length us, event | category | flops | bytes accessed | tf_op | source)
XLA Modules:
  0.0 54.9 jit_solution(445341620953470433)
XLA Ops:
  0.6 52.8 %shard_map.77 = (bf16[256,128]{1,0:T(8,128)(2,1)}, f32[1,256]{1,0:T(1,128)}) custom-call(bf16[256,2048]{1,0:T(8,128)(2,1)} %hidden.1, f32[1,2048]{1,0:T(1,128)} %bitcast.6, bf16[4008,2048]{1,0:T(8,128)(2,1)} %bitcast.5, bf16[16,64128]{1,0:T(8,128)(2,1)} %teacher.1, s32[1,256]{1,0:T(1,128)} %bitcast.7, f32[1,256]{1,0:T(1,128)} %bitcast.8), custom_call_target="tpu_custom_call" | custom-call | flops 8405385216 | bytes 20000000 | tf_op jit(solution)/shard_map/pallas_call | solution.py:440
  53.4 1.5 %shard_map.78 = (bf16[256,128]{1,0:T(8,128)(2,1)}, f32[1,256]{1,0:T(1,128)}) custom-call(bf16[256,128]{1,0:T(8,128)(2,1)} %get-tuple-element.6.grad, f32[1,256]{1,0:T(1,128)} %get-tuple-element.7.loss), custom_call_target="tpu_custom_call" | custom-call | tf_op jit(solution)/shard_map/pallas_call | solution.py:488

commit v7 on v6

--- a/solution.py
+++ b/solution.py
@@ -38,7 +38,7 @@
 def kernel(
     hidden, gain, wt, teacher, labels, cot,
     out, loss,
-    hid, w, t_v, land, feats, logits, fg, g_now, g_next,
+    hid, w, t_v, land, feats, turned_feats, logits, fg, g_now, g_next,
     lse_src, lse_land, st_src, st_land, fin_src, fin_land,
     cx_src, cx_land, rs_src, rs_land,
     a_b, b_b, c_b, l_b, r_b, mx_b, soft_b, hard_b, pick_b, cross_b, inner_b, rows_v,
@@ -195,13 +195,14 @@
     hard_b[...] = zeros
     pick_b[...] = zeros
 
+    turned_feats[...] = feats[...].T
+
     def forward(c):
         for copy in w_copies[c * FWD // BLOCK : (c + 1) * FWD // BLOCK]:
             copy.wait()
-        logits[:, c * FWD : (c + 1) * FWD] = lax.dot_general(
-            feats[...], w[c * FWD : (c + 1) * FWD, :], (((1,), (1,)), ((), ())),
-            preferred_element_type=F32,
-        )
+        logits[:, c * FWD : (c + 1) * FWD] = jnp.dot(
+            w[c * FWD : (c + 1) * FWD, :], turned_feats[...], preferred_element_type=F32
+        ).T
 
     def student_sums(c, s):
         at = slice(s * ROWS, (s + 1) * ROWS)
@@ -235,8 +236,6 @@
         pick_b[at, :] = picked
 
     for c in range(FWDS + 1):
-        if c == 2:
-            send_piece(2)
         if c > 0:
             for s in range(TOK // ROWS):
                 student_sums(c - 1, s)
@@ -261,6 +260,7 @@
 
     pltpu.make_async_copy(st_src, st_land.at[me], mr.at[1]).start()
     lax.fori_loop(1, N, send_stats, 0)
+    send_piece(2)
     send_piece(3)
     send_piece(4)
     wait_for(st_land, mr.at[1])
@@ -451,6 +451,7 @@
             pltpu.VMEM((ROWS, VOCAB), BF16),
             pltpu.VMEM((TOK, PAD + LANES), BF16),
             pltpu.VMEM((TOK, D), BF16),
+            pltpu.VMEM((D, TOK), BF16),
             pltpu.VMEM((TOK, PAD), F32),
             pltpu.VMEM((TOK, D), F32),
             pltpu.VMEM((TOK, BLOCK), BF16),

time: 55.2 us -> 53.2 us (0.964)
  Pallas kernels: 54.2 us -> 52.4 us
    pallas_call x1, Pallas kernels: 52.8 us -> 50.9 us  [on_device(): pl.pallas_call(kernel, out_shape=(jax.ShapeDtypeStruct((TOK, OWN), BF16),...]
where the time goes in v7:
time: 53.2 us; the launch traced here: 53.1 us
  Pallas kernels  52.4 us (98%)
  between operations  0.64 us (1%)
    pallas_call x1, Pallas kernels, on_device(): pl.pallas_call(kernel, out_shape=(jax.ShapeDtypeStruct((TOK, OWN), BF16),...  50.9 us
    pallas_call x1, Pallas kernels, on_device(): pl.pallas_call(finish, out_shape=(jax.ShapeDtypeStruct((TOK, OWN), BF16),...  1.48 us

profile of v7, /device:TPU:1, one launch (start us, length us, event | category | flops | bytes accessed | tf_op | source)
XLA Modules:
  0.0 53.1 jit_solution(2600311397394491526)
XLA Ops:
  0.6 50.9 %shard_map.77 = (bf16[256,128]{1,0:T(8,128)(2,1)}, f32[1,256]{1,0:T(1,128)}) custom-call(bf16[256,2048]{1,0:T(8,128)(2,1)} %hidden.1, f32[1,2048]{1,0:T(1,128)} %bitcast.6, bf16[4008,2048]{1,0:T(8,128)(2,1)} %bitcast.5, bf16[16,64128]{1,0:T(8,128)(2,1)} %teacher.1, s32[1,256]{1,0:T(1,128)} %bitcast.7, f32[1,256]{1,0:T(1,128)} %bitcast.8), custom_call_target="tpu_custom_call" | custom-call | flops 8405385216 | bytes 20000000 | tf_op jit(solution)/shard_map/pallas_call | solution.py:440
  51.6 1.5 %shard_map.78 = (bf16[256,128]{1,0:T(8,128)(2,1)}, f32[1,256]{1,0:T(1,128)}) custom-call(bf16[256,128]{1,0:T(8,128)(2,1)} %get-tuple-element.6.grad, f32[1,256]{1,0:T(1,128)} %get-tuple-element.7.loss), custom_call_target="tpu_custom_call" | custom-call | tf_op jit(solution)/shard_map/pallas_call | solution.py:489

commit v8 on v6

--- a/solution.py
+++ b/solution.py
@@ -20,9 +20,10 @@
 TILES = 32
 PAD = TILES * LANES
 VTILES = VOCAB // LANES
+MOST = TILES + 1
 VALID = SHARD - (TILES - 1) * LANES
-PIECES = ((0, 9), (9, 8), (17, 8), (25, 4), (29, 4))
-FIRST_BLOCK = (0, 2, 4, 6, 7)
+PIECES = ((0, 10), (10, 8), (18, 8), (26, 7))
+FIRST_BLOCK = (0, 2, 4, 6)
 BLOCK = 512
 BLOCKS = PAD // BLOCK
 BLOCK_TILES = BLOCK // LANES
@@ -82,32 +83,28 @@
             device_id={"vocab": d}, device_id_type=MESH,
         )
 
-    def piece_copies(d, c):
+    def first_tile(d):
+        return jnp.minimum(lax.div(d * SHARD, LANES), VTILES - MOST)
+
+    def piece_refs(d, c):
         first, count = PIECES[c]
-        base = lax.div(d * SHARD, LANES)
-        spans = [(base + first, first, count)]
-        if first + count > TILES:
-            spans = [
-                (base + first, first, count - 1),
-                (jnp.minimum(base + TILES, VTILES - 1), TILES, 1),
-            ]
-        for start, at, tiles in spans:
-            yield (
-                teacher.at[:, pl.ds(pl.multiple_of(start * LANES, LANES), tiles * LANES)],
-                land.at[my_rows, at * LANES : (at + tiles) * LANES],
-            )
+        start = pl.multiple_of((first_tile(d) + first) * LANES, LANES)
+        return (
+            teacher.at[:, pl.ds(start, count * LANES)],
+            land.at[my_rows, first * LANES : (first + count) * LANES],
+        )
 
     def send_piece(c):
         for dc in (0, 1):
             for dy, dz in ((0, 1), (1, 0), (3, 0), (2, 1), (1, 1), (2, 0), (3, 1)):
                 d = (lax.rem(z_hi + dz, 2) * 4 + lax.rem(y + dy, 4)) * 2 + lax.rem(core + dc, 2)
-                for src, dst in piece_copies(d, c):
-                    remote(src, dst, ts.at[c], tr.at[c], d).start()
+                src, dst = piece_refs(d, c)
+                remote(src, dst, ts.at[c], tr.at[c], d).start()
         sibling = chip * 2 + (1 - core)
-        for src, dst in piece_copies(sibling, c):
-            remote(src, dst, ts.at[c], tr.at[c], sibling).start()
-        for src, dst in piece_copies(me, c):
-            pltpu.make_async_copy(src, dst, tr.at[c]).start()
+        src, dst = piece_refs(sibling, c)
+        remote(src, dst, ts.at[c], tr.at[c], sibling).start()
+        src, dst = piece_refs(me, c)
+        pltpu.make_async_copy(src, dst, tr.at[c]).start()
 
     send_piece(0)
     for copy in w_copies[2:]:
@@ -235,8 +232,6 @@
         pick_b[at, :] = picked
 
     for c in range(FWDS + 1):
-        if c == 2:
-            send_piece(2)
         if c > 0:
             for s in range(TOK // ROWS):
                 student_sums(c - 1, s)
@@ -261,9 +256,9 @@
 
     pltpu.make_async_copy(st_src, st_land.at[me], mr.at[1]).start()
     lax.fori_loop(1, N, send_stats, 0)
+    send_piece(2)
+    wait_for(st_land, mr.at[1])
     send_piece(3)
-    send_piece(4)
-    wait_for(st_land, mr.at[1])
 
     top = st_land[0, 0:1, :]
     for s in range(1, N):
@@ -299,6 +294,7 @@
     off = lax.rem(me * SHARD, LANES)
     shift = lax.rem(LANES - off, LANES)
     keep = lane < LANES - off
+    skip = lax.div(me * SHARD, LANES) - first_tile(me)
     partner = chip * 2 + (1 - core)
 
     def wait_piece(c):
@@ -314,7 +310,8 @@
         cross, inner = cross_b[at, :], inner_b[at, :]
 
         def turned(i):
-            start = pl.multiple_of(c * BLOCK + i * LANES, LANES)
+            tile = jnp.minimum(c * BLOCK_TILES + i + skip, MOST - 1)
+            start = pl.multiple_of(tile * LANES, LANES)
             return pltpu.roll(land[at, pl.ds(start, LANES)].astype(F32), shift, 1)
 
         here = turned(0)

time: 55.2 us -> 54 us (0.978)
  Pallas kernels: 54.2 us -> 53.2 us
    pallas_call x1, Pallas kernels: 52.8 us -> 51.7 us  [on_device(): pl.pallas_call(kernel, out_shape=(jax.ShapeDtypeStruct((TOK, OWN), BF16),...]
where the time goes in v8:
time: 54 us; the launch traced here: 53.8 us
  Pallas kernels  53.2 us (99%)
  between operations  0.64 us (1%)
    pallas_call x1, Pallas kernels, on_device(): pl.pallas_call(kernel, out_shape=(jax.ShapeDtypeStruct((TOK, OWN), BF16),...  51.7 us
    pallas_call x1, Pallas kernels, on_device(): pl.pallas_call(finish, out_shape=(jax.ShapeDtypeStruct((TOK, OWN), BF16),...  1.48 us

profile of v8, /device:TPU:1, one launch (start us, length us, event | category | flops | bytes accessed | tf_op | source)
XLA Modules:
  0.0 53.8 jit_solution(1779916965750735872)
XLA Ops:
  0.6 51.7 %shard_map.77 = (bf16[256,128]{1,0:T(8,128)(2,1)}, f32[1,256]{1,0:T(1,128)}) custom-call(bf16[256,2048]{1,0:T(8,128)(2,1)} %hidden.1, f32[1,2048]{1,0:T(1,128)} %bitcast.6, bf16[4008,2048]{1,0:T(8,128)(2,1)} %bitcast.5, bf16[16,64128]{1,0:T(8,128)(2,1)} %teacher.1, s32[1,256]{1,0:T(1,128)} %bitcast.7, f32[1,256]{1,0:T(1,128)} %bitcast.8), custom_call_target="tpu_custom_call" | custom-call | flops 8405385216 | bytes 20000000 | tf_op jit(solution)/shard_map/pallas_call | solution.py:437
  52.3 1.5 %shard_map.78 = (bf16[256,128]{1,0:T(8,128)(2,1)}, f32[1,256]{1,0:T(1,128)}) custom-call(bf16[256,128]{1,0:T(8,128)(2,1)} %get-tuple-element.6.grad, f32[1,256]{1,0:T(1,128)} %get-tuple-element.7.loss), custom_call_target="tpu_custom_call" | custom-call | tf_op jit(solution)/shard_map/pallas_call | solution.py:485

commit v9 on v8

--- a/solution.py
+++ b/solution.py
@@ -22,8 +22,8 @@
 VTILES = VOCAB // LANES
 MOST = TILES + 1
 VALID = SHARD - (TILES - 1) * LANES
-PIECES = ((0, 10), (10, 8), (18, 8), (26, 7))
-FIRST_BLOCK = (0, 2, 4, 6)
+PIECES = ((0, 10), (10, 8), (18, 8), (26, 4), (30, 3))
+FIRST_BLOCK = (0, 2, 4, 6, 7)
 BLOCK = 512
 BLOCKS = PAD // BLOCK
 BLOCK_TILES = BLOCK // LANES
@@ -257,8 +257,9 @@
     pltpu.make_async_copy(st_src, st_land.at[me], mr.at[1]).start()
     lax.fori_loop(1, N, send_stats, 0)
     send_piece(2)
+    send_piece(3)
+    send_piece(4)
     wait_for(st_land, mr.at[1])
-    send_piece(3)
 
     top = st_land[0, 0:1, :]
     for s in range(1, N):

time: 54 us -> 53.1 us (0.983)
  Pallas kernels: 53.2 us -> 52.3 us
    pallas_call x1, Pallas kernels: 51.7 us -> 50.8 us  [on_device(): pl.pallas_call(kernel, out_shape=(jax.ShapeDtypeStruct((TOK, OWN), BF16),...]
where the time goes in v9:
time: 53.1 us; the launch traced here: 52.9 us
  Pallas kernels  52.3 us (98%)
  between operations  0.64 us (1%)
    pallas_call x1, Pallas kernels, on_device(): pl.pallas_call(kernel, out_shape=(jax.ShapeDtypeStruct((TOK, OWN), BF16),...  50.8 us
    pallas_call x1, Pallas kernels, on_device(): pl.pallas_call(finish, out_shape=(jax.ShapeDtypeStruct((TOK, OWN), BF16),...  1.48 us

profile of v9, /device:TPU:1, one launch (start us, length us, event | category | flops | bytes accessed | tf_op | source)
XLA Modules:
  0.0 52.9 jit_solution(9658402066725724500)
XLA Ops:
  0.6 50.8 %shard_map.77 = (bf16[256,128]{1,0:T(8,128)(2,1)}, f32[1,256]{1,0:T(1,128)}) custom-call(bf16[256,2048]{1,0:T(8,128)(2,1)} %hidden.1, f32[1,2048]{1,0:T(1,128)} %bitcast.6, bf16[4008,2048]{1,0:T(8,128)(2,1)} %bitcast.5, bf16[16,64128]{1,0:T(8,128)(2,1)} %teacher.1, s32[1,256]{1,0:T(1,128)} %bitcast.7, f32[1,256]{1,0:T(1,128)} %bitcast.8), custom_call_target="tpu_custom_call" | custom-call | flops 8405385216 | bytes 20000000 | tf_op jit(solution)/shard_map/pallas_call | solution.py:438
  51.4 1.5 %shard_map.78 = (bf16[256,128]{1,0:T(8,128)(2,1)}, f32[1,256]{1,0:T(1,128)}) custom-call(bf16[256,128]{1,0:T(8,128)(2,1)} %get-tuple-element.6.grad, f32[1,256]{1,0:T(1,128)} %get-tuple-element.7.loss), custom_call_target="tpu_custom_call" | custom-call | tf_op jit(solution)/shard_map/pallas_call | solution.py:486

commit v10 on v9

--- a/solution.py
+++ b/solution.py
@@ -259,6 +259,9 @@
     send_piece(2)
     send_piece(3)
     send_piece(4)
+    cross_b[...] = zeros
+    inner_b[...] = zeros
+    fg[...] = jnp.zeros((TOK, D), F32)
     wait_for(st_land, mr.at[1])
 
     top = st_land[0, 0:1, :]
@@ -287,9 +290,6 @@
     ).T
     a_b[...] = jnp.broadcast_to(columns[:, 0:1], (TOK, LANES))
     b_b[...] = jnp.broadcast_to(columns[:, 1:2], (TOK, LANES))
-    cross_b[...] = zeros
-    inner_b[...] = zeros
-    fg[...] = jnp.zeros((TOK, D), F32)
     wait_for(lse_land, mr.at[0])
 
     off = lax.rem(me * SHARD, LANES)
@@ -383,14 +383,12 @@
     def own_half(n):
         return half_of(n, core) + cx_land[n].astype(F32)
 
-    def share(k, _):
-        n = lax.rem(chip + 1 + k, CHIPS)
+    for dy, dz in ((2, 1), (2, 0), (1, 1), (3, 0), (3, 1), (1, 0), (0, 1)):
+        n = lax.rem(z_hi + dz, 2) * 4 + lax.rem(y + dy, 4)
         wait_for(cx_land.at[n], cr.at[n])
         rs_src[n] = own_half(n).astype(BF16)
         remote(rs_src.at[n], rs_land.at[chip], rs, rr, n * 2 + core).start()
-        return 0
-
-    lax.fori_loop(0, CHIPS - 1, share, 0)
+
     wait_for(cx_land.at[chip], cr.at[chip])
 
     wait_for(fin_land, mr.at[2])

time: 53.1 us -> 53.8 us (1.013)
  Pallas kernels: 52.3 us -> 52.9 us
    pallas_call x1, Pallas kernels: 50.8 us -> 51.5 us  [on_device(): pl.pallas_call(kernel, out_shape=(jax.ShapeDtypeStruct((TOK, OWN), BF16),...]
where the time goes in v10:
time: 53.8 us; the launch traced here: 53.6 us
  Pallas kernels  52.9 us (98%)
  between operations  0.64 us (1%)
    pallas_call x1, Pallas kernels, on_device(): pl.pallas_call(kernel, out_shape=(jax.ShapeDtypeStruct((TOK, OWN), BF16),...  51.5 us
    pallas_call x1, Pallas kernels, on_device(): pl.pallas_call(finish, out_shape=(jax.ShapeDtypeStruct((TOK, OWN), BF16),...  1.48 us

profile of v10, /device:TPU:1, one launch (start us, length us, event | category | flops | bytes accessed | tf_op | source)
XLA Modules:
  0.0 53.6 jit_solution(11700938339221740969)
XLA Ops:
  0.6 51.5 %shard_map.77 = (bf16[256,128]{1,0:T(8,128)(2,1)}, f32[1,256]{1,0:T(1,128)}) custom-call(bf16[256,2048]{1,0:T(8,128)(2,1)} %hidden.1, f32[1,2048]{1,0:T(1,128)} %bitcast.6, bf16[4008,2048]{1,0:T(8,128)(2,1)} %bitcast.5, bf16[16,64128]{1,0:T(8,128)(2,1)} %teacher.1, s32[1,256]{1,0:T(1,128)} %bitcast.7, f32[1,256]{1,0:T(1,128)} %bitcast.8), custom_call_target="tpu_custom_call" | custom-call | flops 8405385216 | bytes 20000000 | tf_op jit(solution)/shard_map/pallas_call | solution.py:436
  52.1 1.5 %shard_map.78 = (bf16[256,128]{1,0:T(8,128)(2,1)}, f32[1,256]{1,0:T(1,128)}) custom-call(bf16[256,128]{1,0:T(8,128)(2,1)} %get-tuple-element.6.grad, f32[1,256]{1,0:T(1,128)} %get-tuple-element.7.loss), custom_call_target="tpu_custom_call" | custom-call | tf_op jit(solution)/shard_map/pallas_call | solution.py:484
